TPU v7x, 128 devices: a whole 4x4x4 slice. The times are simulated.
128 devices in a mesh: dp: 4 (over z_hi, core), ctx: 32 (over y, z_lo, x).
Axes of the slice: x: 4, y: 4, z: 4 (z_hi: 2, z_lo: 2; z = z_hi * 2 + z_lo), core: 2. Of those that a mesh axis runs over, the one named last changes fastest.
Arguments:
- query_rows: bfloat16 [16384, 8192], P(('dp', 'ctx')), parts along dimension 0, may hold values from -6 to 6
- key_rows: bfloat16 [16384, 8192], P(('dp', 'ctx')), parts along dimension 0, may hold values from -6 to 6
- value_rows: bfloat16 [16384, 8192], P(('dp', 'ctx')), parts along dimension 0, may hold values from -6 to 6
- short_taps: float32 [3, 3, 8192], replicated, may hold values from -3.5 to 3.5
- long_filter: float32 [4096, 8192], P(None, 'ctx'), may hold values from -0.09375 to 0.09375
- skip_gain: float32 [8192], P('ctx'), may hold values from 0.5 to 1.5
Outputs:
- mixed: bfloat16 [16384, 8192], P(('dp', 'ctx')), parts along dimension 0
There are 4 independent parts, one for each index of `dp`. A program takes and returns all parts, laid end to end along the dimension named above; an argument that names none is the same for every part. Nothing has to cross between parts.
All inputs are finite; a program needn't handle non-finite values.
Results may differ from a plain program's by a relative error of at most 0.0058.
Values may be sent and summed in bfloat16 or wider, within the bound.
A program may use at most 192 MiB of HBM per device.

v0:
```python
import math

import jax
import jax.numpy as jnp
from jax import lax
from jax.sharding import PartitionSpec as P

TAPS = 3


def shifted(block, axis, distance):
    devices = range(lax.axis_size(axis))
    route = [(i - distance, i) for i in devices if i - distance in devices]
    return lax.ppermute(block, axis, route)


def featurize(signal, edge, tap_weights):
    row_count = signal.shape[0]
    widened = jnp.concatenate([edge, signal], axis=0).astype(jnp.float32)
    result = jnp.zeros(signal.shape, jnp.float32)
    for offset in range(TAPS):
        result = (
            result
            + tap_weights[offset] * widened[TAPS - 1 - offset : TAPS - 1 - offset + row_count]
        )
    return result


def angle_tables(modulus, rows_n, cols_n):
    product = (
        jnp.arange(rows_n, dtype=jnp.int32)[:, None]
        * jnp.arange(cols_n, dtype=jnp.int32)[None, :]
        % modulus
    )
    angle = product.astype(jnp.float32) * (2.0 * math.pi / modulus)
    return (jnp.cos(angle), jnp.sin(angle))


def contract(form, table, grid):
    return jnp.einsum(form, table, grid, precision=lax.Precision.HIGHEST)


def forward_spectrum(signal, half_outer, inner_len, tables):
    outer_first, inner_pair, twist_cos, twist_sin, outer_last = tables
    grid = signal.reshape(half_outer, inner_len, signal.shape[1])
    parts = contract("pkn,nmc->pkmc", outer_first, grid)
    turned = jnp.stack(
        [
            parts[0] * twist_cos[:, :, None] + parts[1] * twist_sin[:, :, None],
            parts[1] * twist_cos[:, :, None] - parts[0] * twist_sin[:, :, None],
        ]
    )
    return jnp.einsum("pqln,qknc->pklc", inner_pair, turned, precision=lax.Precision.HIGHEST)


def inverse_real(spectrum, tables):
    outer_first, inner_pair, twist_cos, twist_sin, outer_last = tables
    inner_back = jnp.stack(
        [
            jnp.stack([inner_pair[0, 0], -inner_pair[0, 1]]),
            jnp.stack([-inner_pair[1, 0], inner_pair[1, 1]]),
        ]
    )
    back = jnp.einsum("pqnl,qklc->pknc", inner_back, spectrum, precision=lax.Precision.HIGHEST)
    turned = jnp.stack(
        [
            back[0] * twist_cos[:, :, None] - back[1] * twist_sin[:, :, None],
            back[1] * twist_cos[:, :, None] + back[0] * twist_sin[:, :, None],
        ]
    )
    return jnp.einsum("pnk,pkmc->nmc", outer_last, turned, precision=lax.Precision.HIGHEST)


def long_convolve(gated, filter_part, skip_part):
    seq_length, chan_count = gated.shape
    full_len = 2 * seq_length
    outer_len = 2
    for divisor in range(2, full_len + 1, 2):
        if full_len % divisor == 0 and divisor * divisor <= full_len:
            outer_len = divisor
    inner_len = full_len // outer_len
    half_outer = outer_len // 2
    cos_outer, sin_outer = angle_tables(outer_len, outer_len, outer_len)
    cos_inner, sin_inner = angle_tables(inner_len, inner_len, inner_len)
    twist_cos, twist_sin = angle_tables(full_len, outer_len, inner_len)
    outer_first = jnp.stack([cos_outer[:, :half_outer], -sin_outer[:, :half_outer]])
    inner_pair = jnp.stack([jnp.stack([cos_inner, sin_inner]), jnp.stack([-sin_inner, cos_inner])])
    outer_last = jnp.stack([cos_outer[:half_outer], -sin_outer[:half_outer]])
    tables = (outer_first, inner_pair, twist_cos, twist_sin, outer_last)
    gated_wide = gated.astype(jnp.float32)
    signal_spec = forward_spectrum(gated_wide, half_outer, inner_len, tables)
    kernel_spec = forward_spectrum(filter_part, half_outer, inner_len, tables)
    product = jnp.stack(
        [
            signal_spec[0] * kernel_spec[0] - signal_spec[1] * kernel_spec[1],
            signal_spec[0] * kernel_spec[1] + signal_spec[1] * kernel_spec[0],
        ]
    )
    restored = inverse_real(product, tables).reshape(seq_length, chan_count)
    convolved = restored * (1.0 / full_len) + skip_part * gated_wide
    return convolved.astype(jnp.bfloat16)


def on_device(query_rows, key_rows, value_rows, short_taps, long_filter, skip_gain):
    row_count, total_width = query_rows.shape
    device_count = lax.axis_size("ctx")
    chan_count = total_width // device_count
    query_edge = shifted(query_rows[row_count - (TAPS - 1) :], "ctx", 1)
    featured_q = featurize(query_rows, query_edge, short_taps[0])
    moved_k, moved_v = (
        lax.all_to_all(
            key_rows.reshape(row_count, device_count, chan_count),
            "ctx",
            split_axis=1,
            concat_axis=0,
            tiled=True,
        ),
        lax.all_to_all(
            value_rows.reshape(row_count, device_count, chan_count),
            "ctx",
            split_axis=1,
            concat_axis=0,
            tiled=True,
        ),
    )
    first_chan = lax.axis_index("ctx") * chan_count
    taps_k = lax.dynamic_slice_in_dim(short_taps[1], first_chan, chan_count, 1)
    taps_v = lax.dynamic_slice_in_dim(short_taps[2], first_chan, chan_count, 1)
    zero_edge = jnp.zeros((TAPS - 1, chan_count), jnp.bfloat16)
    seq_length = row_count * device_count
    featured_k = featurize(moved_k.reshape(seq_length, chan_count), zero_edge, taps_k)
    featured_v = featurize(moved_v.reshape(seq_length, chan_count), zero_edge, taps_v)
    gated = (featured_k * featured_v).astype(jnp.bfloat16)
    conv_out = long_convolve(gated, long_filter, skip_gain)
    returned = lax.all_to_all(
        conv_out.reshape(row_count * device_count, 1, chan_count),
        "ctx",
        split_axis=0,
        concat_axis=1,
        tiled=True,
    )
    return (featured_q * returned.reshape(row_count, total_width).astype(jnp.float32)).astype(
        jnp.bfloat16
    )


def solution(mesh):
    in_specs = (
        P(("dp", "ctx"), None),
        P(("dp", "ctx"), None),
        P(("dp", "ctx"), None),
        P(),
        P(None, "ctx"),
        P("ctx"),
    )
    out_specs = P(("dp", "ctx"), None)
    return jax.shard_map(
        on_device, mesh=mesh, in_specs=in_specs, out_specs=out_specs, check_vma=False
    )
```

profile of v0, /device:TPU:1, one launch (start us, length us, event | category | flops | bytes accessed | tf_op | source)
XLA Modules:
  0.0 354.8 jit_solution(8695905275239394294)
XLA Ops:
  0.0 4.1 %copy.39 = bf16[128,8192]{0,1:T(8,128)(2,1)} copy(bf16[128,8192]{1,0:T(8,128)(2,1)} %param.7) | data formatting | bytes 4194304 | tf_op args[1]
  4.1 9.2 %all-to-all-start = ((bf16[128,32,256]{0,2,1:T(8,128)(2,1)}), bf16[128,32,256]{0,2,1:T(8,128)(2,1)S(1)}, u32[]{:S(2)}, u32[]{:S(2)}) async-start(bf16[128,32,256]{0,2,1:T(8,128)(2,1)} %bitcast.123), calls=%async_computation | async-start | bytes 4194304 | tf_op jit(solution)/shard_map/all_to_all | solution.py:111
  14.3 3.1 collective-permute-start
  17.7 4.1 %copy.41 = bf16[128,8192]{0,1:T(8,128)(2,1)} copy(bf16[128,8192]{1,0:T(8,128)(2,1)} %param.8) | data formatting | bytes 4194304 | tf_op args[2]
  22.4 17.9 %all-to-all-done = bf16[128,32,256]{0,2,1:T(8,128)(2,1)S(1)} async-done(((bf16[128,32,256]{0,2,1:T(8,128)(2,1)}), bf16[128,32,256]{0,2,1:T(8,128)(2,1)S(1)}, u32[]{:S(2)}, u32[]{:S(2)}) %all-to-all-start) | async-done | bytes 2097184 | tf_op jit(solution)/shard_map/all_to_all | solution.py:111
  40.3 7.0 %all-to-all-start.1 = ((bf16[128,32,256]{0,2,1:T(8,128)(2,1)}), bf16[128,32,256]{0,2,1:T(8,128)(2,1)}, u32[]{:S(2)}, u32[]{:S(2)}) async-start(bf16[128,32,256]{0,2,1:T(8,128)(2,1)} %bitcast.122), calls=%async_computation.1 | async-start | bytes 4194304 | tf_op jit(solution)/shard_map/all_to_all | solution.py:118
  48.0 19.1 %fusion.29 = f32[2,64,128,256]{3,1,2,0:T(8,128)} fusion(f32[32,128,256]{2,1,0:T(8,128)} %bitcast.118, f32[1,64,32]{1,2,0:T(8,128)S(1)} %get-tuple-element.37, f32[1,64,32]{1,2,0:T(8,128)S(1)} %get-tuple-element.38), kind=kOutput, calls=%fused_computation.49 | convolution fusion | flops 1610616832 | bytes 20987904 | tf_op jit(solution)/shard_map/pkn,nmc->pkmc/dot_general | solution.py:40
  67.1 2.9 copy.40
  70.0 3.4 all-to-all-done.1
  73.4 3.3 copy.42
  79.1 2.8 fusion.20
  81.9 11.0 %fusion.34 = f32[2,64,128,256]{3,1,2,0:T(8,128)} fusion(bf16[32,128,256]{2,1,0:T(8,128)(2,1)S(1)} %bitcast.117, f32[1,64,32]{1,2,0:T(8,128)S(1)} %get-tuple-element.37, f32[1,64,32]{1,2,0:T(8,128)S(1)} %get-tuple-element.38), kind=kOutput, calls=%fused_computation.54 | convolution fusion | flops 1610616832 | bytes 18890752 | tf_op jit(solution)/shard_map/pkn,nmc->pkmc/dot_general | solution.py:40
  93.0 16.9 %multiply_add_fusion.3 = (f32[1,64,128,256]{3,1,2,0:T(8,128)}, f32[1,64,128,256]{3,1,2,0:T(8,128)}, f32[1,64,128,256]{3,1,2,0:T(8,128)}, f32[1,64,128,256]{3,1,2,0:T(8,128)}) fusion(f32[2,64,128,256]{3,1,2,0:T(8,128)} %fusion.34, f32[64,128]{0,1:T(8,128)S(1)} %get-tuple-element.39, f32[64,128]{0,1:T(8,128)S(1)} %get-tuple-element.40, ...), kind=kLoop, calls=%fused_computation.24 | loop fusion | flops 25165824 | bytes 67174400 | tf_op jit(solution)/shard_map/add | solution.py:49
  109.9 7.3 %maximum_bitcast_fusion = f32[2,64,128,256,1]{3,1,2,0,4:T(8,128)S(1)} fusion(f32[1,64,128,256]{3,1,2,0:T(8,128)} %get-tuple-element.10, f32[1,64,128,256]{3,1,2,0:T(8,128)} %get-tuple-element.9), kind=kLoop, calls=%fused_computation | loop fusion | flops 4194304 | bytes 33554432 | tf_op jit(solution)/shard_map/stack | solution.py:47
  117.2 42.3 %fusion.11 = f32[2,64,128,256]{2,3,0,1:T(8,128)} fusion(f32[2,64,128,256,1]{3,1,2,0,4:T(8,128)S(1)} %maximum_bitcast_fusion, f32[1,2,128,128]{3,2,1,0:T(8,128)S(1)} %get-tuple-element.31, f32[1,2,128,128]{3,2,1,0:T(8,128)S(1)} %get-tuple-element.30), kind=kOutput, calls=%fused_computation.14 | convolution fusion | flops 12884967424 | bytes 33816576 | tf_op jit(solution)/shard_map/pqln,qknc->pklc/dot_general | solution.py:53
  161.6 42.6 %fusion.14 = f32[2,64,128,256]{2,3,0,1:T(8,128)} fusion(f32[2,64,128,256,1]{3,1,2,0,4:T(8,128)S(1)} %maximum_bitcast_fusion.1, f32[1,2,128,128]{3,2,1,0:T(8,128)S(1)} %get-tuple-element.31, f32[1,2,128,128]{3,2,1,0:T(8,128)S(1)} %get-tuple-element.30), kind=kOutput, calls=%fused_computation.15 | convolution fusion | flops 12884967424 | bytes 33816576 | tf_op jit(solution)/shard_map/pqln,qknc->pklc/dot_general | solution.py:53
  204.2 19.5 %multiply_subtract_fusion.1 = (f32[1,64,128,256]{2,3,0,1:T(8,128)}, f32[1,64,128,256]{2,3,0,1:T(8,128)}) fusion(f32[2,64,128,256]{2,3,0,1:T(8,128)} %fusion.14, f32[2,64,128,256]{2,3,0,1:T(8,128)} %fusion.11), kind=kLoop, calls=%fused_computation.20 | loop fusion | flops 12582912 | bytes 50331648 | tf_op jit(solution)/shard_map/sub | solution.py:95
  223.7 18.5 %fusion.17 = f32[64,256,2,128]{3,1,2,0:T(8,128)} fusion(f32[1,64,128,256]{2,3,0,1:T(8,128)} %get-tuple-element.6, f32[1,64,128,256]{2,3,0,1:T(8,128)} %get-tuple-element.5, f32[1,2,128,128]{3,2,1,0:T(8,128)S(1)} %maximum_bitcast_fusion.14, f32[1,2,128,128]{3,2,1,0:T(8,128)S(1)} %maximum_bitcast_fusion.13), kind=kOutput, calls=%fused_computation.16 | convolution fusion | flops 12889161728 | bytes 33816576 | tf_op jit(solution)/shard_map/pqnl,qklc->pknc/dot_general | solution.py:64
  242.1 17.5 %copy.47 = f32[64,256,2,128]{1,0,3,2:T(8,128)} copy(f32[64,256,2,128]{3,1,2,0:T(8,128)} %fusion.17) | data formatting | bytes 33554432 | tf_op jit(solution)/shard_map/pqnl,qklc->pknc/dot_general | solution.py:64
  259.6 8.7 %multiply_subtract_fusion = (f32[1,64,128,256]{3,1,2,0:T(8,128)S(1)}, f32[1,64,128,256]{3,1,2,0:T(8,128)S(1)}) fusion(f32[2,64,128,256]{3,1,2,0:T(8,128)} %bitcast.112, f32[64,128]{0,1:T(8,128)S(1)} %get-tuple-element.39, f32[64,128]{0,1:T(8,128)S(1)} %get-tuple-element.40), kind=kLoop, calls=%fused_computation.18 | loop fusion | flops 12582912 | bytes 33619968 | tf_op jit(solution)/shard_map/sub | solution.py:67
  268.3 9.6 %bitcast_multiply_fusion = f32[32,128,256]{2,0,1:T(8,128)S(1)} fusion(f32[1,64,128,256]{3,1,2,0:T(8,128)S(1)} %get-tuple-element.8, f32[1,64,128,256]{3,1,2,0:T(8,128)S(1)} %get-tuple-element.7, f32[1,32,64]{1,2,0:T(8,128)S(1)} %get-tuple-element.43, f32[1,32,64]{1,2,0:T(8,128)S(1)} %get-tuple-element.44), kind=kOutput, calls=%fused_computation.44 | convolution fusion | flops 1615859712 | bytes 20987904 | tf_op jit(solution)/shard_map/pnk,pkmc->nmc/dot_general | solution.py:71
  282.1 3.0 reduce
  285.1 4.0 %reshape.211 = bf16[32,2,16384]{2,1,0:T(2,128)(2,1)} reshape(bf16[4096,256]{1,0:T(8,128)(2,1)} %reduce) | data formatting | bytes 4194304
  289.1 7.4 %all-to-all-start.2 = ((bf16[32,2,16384]{2,1,0:T(2,128)(2,1)}), bf16[32,2,16384]{2,1,0:T(2,128)(2,1)S(1)}, u32[]{:S(2)}, u32[]{:S(2)}) async-start(bf16[32,2,16384]{2,1,0:T(2,128)(2,1)} %reshape.211), calls=%async_computation.2 | async-start | bytes 4194304 | tf_op jit(solution)/shard_map/all_to_all | solution.py:135
  296.6 4.1 %copy.38 = bf16[128,8192]{0,1:T(8,128)(2,1)} copy(bf16[128,8192]{1,0:T(8,128)(2,1)} %param.6) | data formatting | bytes 4194304 | tf_op args[0]
  302.5 7.0 %maximum_convert_fusion = f32[130,8192]{0,1:T(8,128)} fusion(bf16[128,8192]{0,1:T(8,128)(2,1)} %copy.38, bf16[2,8192]{0,1:T(8,128)(2,1)} %copy.37), kind=kLoop, calls=%fused_computation.45 | loop fusion | flops 4259840 | bytes 6389760 | tf_op jit(solution)/shard_map/convert_element_type | solution.py:19
  309.5 12.7 %all-to-all-done.2 = bf16[32,2,16384]{2,1,0:T(2,128)(2,1)S(1)} async-done(((bf16[32,2,16384]{2,1,0:T(2,128)(2,1)}), bf16[32,2,16384]{2,1,0:T(2,128)(2,1)S(1)}, u32[]{:S(2)}, u32[]{:S(2)}) %all-to-all-start.2) | async-done | bytes 2097184 | tf_op jit(solution)/shard_map/all_to_all | solution.py:135
  322.2 6.8 %reshape.212 = bf16[4096,1,256]{2,1,0:T(2,128)(2,1)} reshape(bf16[32,2,16384]{2,1,0:T(2,128)(2,1)S(1)} %all-to-all-done.2) | data formatting | bytes 4194304
  328.9 2.5 copy.52
  333.9 5.6 %copy.53 = f32[128,32,1,256]{0,3,1,2:T(8,128)} copy(f32[128,32,1,256]{3,0,1,2:T(8,128)} %convert_bitcast_fusion) | data formatting | bytes 8388608 | tf_op jit(solution)/shard_map/convert_element_type | solution.py:142
  339.5 12.1 %fusion.26 = bf16[128,8192]{0,1:T(8,128)(2,1)S(1)} fusion(f32[130,8192]{0,1:T(8,128)} %maximum_convert_fusion, f32[128,32,1,256]{0,3,1,2:T(8,128)} %copy.53, f32[8192]{0:T(1024)S(1)} %bitcast.127, f32[8192]{0:T(1024)S(1)} %bitcast.128, f32[8192]{0:T(1024)S(1)} %bitcast.126), kind=kLoop, calls=%fused_computation.40 | loop fusion | flops 7340032 | bytes 18972672 | tf_op jit(solution)/shard_map/convert_element_type | solution.py:142
  351.7 2.9 copy.54
  (51 shorter events, 15.5 us)
Async XLA Ops:
  0.0 22.3 %copy-start.2 = (f32[3,3,8192]{2,1,0:T(4,128)S(1)}, f32[3,3,8192]{2,1,0:T(4,128)}, u32[]{:S(2)}) copy-start(f32[3,3,8192]{2,1,0:T(4,128)} %param.9) | copy-start | bytes 884740
  4.1 36.2 %all-to-all-start = ((bf16[128,32,256]{0,2,1:T(8,128)(2,1)}), bf16[128,32,256]{0,2,1:T(8,128)(2,1)S(1)}, u32[]{:S(2)}, u32[]{:S(2)}) async-start(bf16[128,32,256]{0,2,1:T(8,128)(2,1)} %bitcast.123), calls=%async_computation | async-start | bytes 4194304 | tf_op jit(solution)/shard_map/all_to_all | solution.py:111
  14.3 286.4 %collective-permute-start = (bf16[2,8192]{1,0:T(2,128)(2,1)S(1)}, bf16[2,8192]{1,0:T(2,128)(2,1)S(1)}, u32[]{:S(2)}, u32[]{:S(2)}) collective-permute-start(bf16[2,8192]{1,0:T(2,128)(2,1)S(1)} %slice.141), channel_id=1, source_target_pairs={{0,1},{1,2},{2,3},{3,4},{4,5},{5,6},{6,7},{7,8},{8,9},{9,10},{10,1... | collective-permute-start | bytes 98312 | tf_op jit(solution)/shard_map/ppermute | solution.py:14
  40.3 33.1 %all-to-all-start.1 = ((bf16[128,32,256]{0,2,1:T(8,128)(2,1)}), bf16[128,32,256]{0,2,1:T(8,128)(2,1)}, u32[]{:S(2)}, u32[]{:S(2)}) async-start(bf16[128,32,256]{0,2,1:T(8,128)(2,1)} %bitcast.122), calls=%async_computation.1 | async-start | bytes 4194304 | tf_op jit(solution)/shard_map/all_to_all | solution.py:118
  79.1 13.8 %slice-start = ((s8[16777216]{0:T(1024)(128)(4,1)}), s8[4194304]{0:T(1024)(128)(4,1)S(1)}, s32[]{:S(2)}) async-start(s8[16777216]{0:T(1024)(128)(4,1)} %bitcast.110), calls=%async_computation.3 | async-start | bytes 8388608
  79.1 13.8 %slice-start.1 = ((s8[16777216]{0:T(1024)(128)(4,1)}), s8[4194304]{0:T(1024)(128)(4,1)S(1)}, s32[]{:S(2)}) async-start(s8[16777216]{0:T(1024)(128)(4,1)} %bitcast.110), calls=%async_computation.4 | async-start | bytes 8388608
  79.1 13.8 %slice-start.2 = ((s8[16777216]{0:T(1024)(128)(4,1)}), s8[4194304]{0:T(1024)(128)(4,1)S(1)}, s32[]{:S(2)}) async-start(s8[16777216]{0:T(1024)(128)(4,1)} %bitcast.110), calls=%async_computation.5 | async-start | bytes 8388608
  81.9 11.0 %copy-start = (bf16[4096,256]{1,0:T(8,128)(2,1)}, bf16[4096,256]{1,0:T(8,128)(2,1)S(1)}, u32[]{:S(2)}) copy-start(bf16[4096,256]{1,0:T(8,128)(2,1)S(1)} %fusion.20) | copy-start | bytes 6291460
  81.9 11.0 %slice-start.3 = ((s8[16777216]{0:T(1024)(128)(4,1)}), s8[4194304]{0:T(1024)(128)(4,1)S(1)}, s32[]{:S(2)}) async-start(s8[16777216]{0:T(1024)(128)(4,1)} %bitcast.110), calls=%async_computation.6 | async-start | bytes 8388608
  109.9 49.7 %slice-start.4 = ((s8[8388608]{0:T(1024)(128)(4,1)}), s8[4194304]{0:T(1024)(128)(4,1)S(1)}, s32[]{:S(2)}) async-start(s8[8388608]{0:T(1024)(128)(4,1)} %bitcast.113), calls=%async_computation.7 | async-start | bytes 8388608
  109.9 49.7 %slice-start.6 = ((s8[8388608]{0:T(1024)(128)(4,1)}), s8[4194304]{0:T(1024)(128)(4,1)S(1)}, s32[]{:S(2)}) async-start(s8[8388608]{0:T(1024)(128)(4,1)} %bitcast.115), calls=%async_computation.9 | async-start | bytes 8388608
  117.2 42.4 %slice-start.5 = ((s8[8388608]{0:T(1024)(128)(4,1)}), s8[4194304]{0:T(1024)(128)(4,1)S(1)}, s32[]{:S(2)}) async-start(s8[8388608]{0:T(1024)(128)(4,1)} %bitcast.113), calls=%async_computation.8 | async-start | bytes 8388608
  117.2 42.4 %slice-start.7 = ((s8[8388608]{0:T(1024)(128)(4,1)}), s8[4194304]{0:T(1024)(128)(4,1)S(1)}, s32[]{:S(2)}) async-start(s8[8388608]{0:T(1024)(128)(4,1)} %bitcast.115), calls=%async_computation.10 | async-start | bytes 8388608
  277.9 2.5 copy-start.1
  277.9 2.5 copy-start.3
  289.1 33.1 %all-to-all-start.2 = ((bf16[32,2,16384]{2,1,0:T(2,128)(2,1)}), bf16[32,2,16384]{2,1,0:T(2,128)(2,1)S(1)}, u32[]{:S(2)}, u32[]{:S(2)}) async-start(bf16[32,2,16384]{2,1,0:T(2,128)(2,1)} %reshape.211), calls=%async_computation.2 | async-start | bytes 4194304 | tf_op jit(solution)/shard_map/all_to_all | solution.py:135
where the time goes:
time: 361 us; the launch traced here: 355 us
  matrix products  143 us (40%)
  other arithmetic  86.6 us (24%)
  local copies, waits for them, and re-layouts  63.8 us (18%)
  waiting for transfers between devices  33.9 us (9%)
  starting transfers between devices  26.7 us (7%)
    dot_general x2, matrix products, forward_spectrum(): jnp.einsum('pqln,qknc->pklc', inner_pair, turned, precision=lax.Precision...  84.9 us
    dot_general x2, matrix products, contract(): return jnp.einsum(form, table, grid, precision=lax.Precision.HIGHEST)  30.1 us
    unnamed x29, local copies, waits for them, and re-layouts  23.1 us
    sub x1, other arithmetic, long_convolve(): signal_spec[0] * kernel_spec[0] - signal_spec[1] * kernel_spec[1]  19.5 us
    dot_general x1, matrix products, inverse_real(): jnp.einsum('pqnl,qklc->pknc', inner_back, spectrum, precision=lax.Precisi...  18.5 us
    all_to_all x1, waiting for transfers between devices, on_device(): lax.all_to_all(key_rows.reshape(row_count, device_count, chan_count), 'ct...  17.9 us
    dot_general x1, local copies, waits for them, and re-layouts, inverse_real(): jnp.einsum('pqnl,qklc->pknc', inner_back, spectrum, precision=lax.Precisi...  17.5 us
    add x1, other arithmetic, forward_spectrum(): parts[0] * twist_cos[:, :, None] + parts[1] * twist_sin[:, :, None]  16.9 us
  transfers between devices with their start and end apart: 4, of which 3 were waited for; matrix products, arithmetic and copies ran while one was open for 72% of the time, Pallas kernels for 0%

commit v1 on v0

v1 whole, which is shorter than its diff:
```python
import functools

import jax
import jax.numpy as jnp
import ml_dtypes
import numpy as np
from jax import lax
from jax.experimental import pallas as pl
from jax.experimental.pallas import tpu as pltpu
from jax.sharding import PartitionSpec as P

F32, BF16 = jnp.float32, jnp.bfloat16
MESH = pl.DeviceIdType.MESH

BLOCKS, ROWS, LANES = 32, 128, 128
FULL = 2 * BLOCKS * ROWS
HALVES = 2


def transform_tables():
    p, k1 = np.arange(BLOCKS), np.arange(BLOCKS)
    angle = 2 * np.pi * (k1[:, None] * p % 64) / 64
    outer = np.zeros((BLOCKS, 2, BLOCKS))
    outer[:, 0], outer[:, 1] = np.cos(angle), -np.sin(angle)
    outer[0, 1] = np.cos(np.pi * p)
    outer_back = np.zeros((BLOCKS, BLOCKS, 2))
    outer_back[:, :, 0], outer_back[:, :, 1] = 2 * np.cos(angle.T), -2 * np.sin(angle.T)
    outer_back[:, 0, 0], outer_back[:, 0, 1] = 1, np.cos(np.pi * p)
    outer_back /= FULL
    r, k2 = np.arange(ROWS), np.arange(ROWS)
    inner = np.zeros((BLOCKS, 2 * ROWS, 2 * ROWS))
    for k in range(1, BLOCKS):
        turn = 2 * np.pi * ((k + 64 * k2)[:, None] * r % FULL) / FULL
        cos, sin = np.cos(turn), np.sin(turn)
        inner[k] = np.block([[cos, sin], [-sin, cos]])
    half = np.arange(64)[:, None]
    even = 2 * np.pi * (64 * half * r % FULL) / FULL
    odd = 2 * np.pi * ((32 + 64 * half) * r % FULL) / FULL
    inner[0, 0:64, :ROWS], inner[0, 64:128, ROWS:] = np.cos(even), np.cos(odd)
    inner[0, 128:192, :ROWS], inner[0, 192:256, ROWS:] = -np.sin(even), -np.sin(odd)
    inner[0, 128, :ROWS] = np.cos(np.pi * r)
    inner_back = inner.transpose(0, 2, 1).copy()
    weight = np.full(2 * ROWS, 2.0)
    weight[0] = weight[128] = 1
    inner_back[0] *= weight
    eye = np.eye(8)
    outer = np.kron(outer.reshape(2 * BLOCKS, BLOCKS), eye)
    outer_back = np.kron(outer_back.reshape(BLOCKS, 2 * BLOCKS), eye)
    return outer, inner, inner_back, outer_back


def high_low(table):
    table = table.astype(np.float32)
    high = table.astype(ml_dtypes.bfloat16)
    return np.stack([high, (table - high.astype(np.float32)).astype(ml_dtypes.bfloat16)])


def high(table):
    return table.astype(np.float32).astype(ml_dtypes.bfloat16)


def dot(a, b):
    return jnp.dot(a, b, preferred_element_type=F32)


def split(a):
    top = a.astype(BF16)
    return top, (a - top.astype(F32)).astype(BF16)


def side_by_side(x, n):
    return jnp.concatenate([x[:, :8].reshape(8 * n, LANES), x[:, 8:].reshape(8 * n, LANES)], axis=1)


def stacked(z, n):
    return jnp.concatenate([z[:, :LANES].reshape(n, 8, LANES), z[:, LANES:].reshape(n, 8, LANES)], axis=1)


def loop(count, step, body):
    def several(j, carry):
        for i in range(step):
            body(j * step + i)
        return carry

    lax.fori_loop(0, count // step, several, 0)


def featurize(block, taps, edge_two, edge_one):
    row = lax.broadcasted_iota(jnp.int32, (8, LANES), 0)
    one, two = pltpu.roll(block, 1, 0), pltpu.roll(block, 2, 0)
    top_one = jnp.where(row == 0, edge_one, one[:8])
    top_two = jnp.where(row == 0, edge_two, jnp.where(row == 1, edge_one, two[:8]))
    one = jnp.concatenate([top_one, one[8:]], axis=0)
    two = jnp.concatenate([top_two, two[8:]], axis=0)
    return taps[0] * block + taps[1] * one + taps[2] * two


def kernel(
    query, key, value, short_taps, filt, skip, outer, inner, inner_back, outer_back, out,
    qbuf, kbuf, vbuf, taps, fbuf, sbuf, t_outer, t_inner, t_inner_back, t_outer_back,
    kv_out, kv_in, q_out, q_in, edges, gated, moved, conv, back,
    spec, spec_low, fspec, mid, featured, result,
    load_sem, edge_send, edge_recv, send_one, recv_one, send_two, recv_two, store_sem,
):
    me = lax.axis_index("ctx")
    x, z, y = me % 4, (me // 4) % 2, me // 8

    def partner(j):
        j = 31 - j
        dx, dz, dy = (j % 4), (j // 4) % 2, j // 8
        return (((y + dy) % 4) * 2 + (z + dz) % 2) * 4 + (x + dx) % 4

    barrier = pltpu.get_barrier_semaphore()

    def greet(j, carry):
        pl.semaphore_signal(barrier, inc=1, device_id={"ctx": (me + j) % BLOCKS}, device_id_type=MESH)
        return carry

    lax.fori_loop(1, BLOCKS, greet, 0)

    loads = [
        pltpu.make_async_copy(src, dst, load_sem.at[i])
        for i, (src, dst) in enumerate(
            [
                (key, kbuf), (value, vbuf), (query, qbuf), (short_taps, taps), (filt, fbuf), (outer, t_outer),
                (inner, t_inner), (skip, sbuf), (inner_back, t_inner_back), (outer_back, t_outer_back),
            ]
        )
    ]
    for load in loads:
        load.start()
    for i in (0, 1, 2):
        loads[i].wait()

    def last_rows(buf):
        return buf[ROWS - 16 :, :].astype(F32)[14:16]

    last_k, last_v, last_q = last_rows(kbuf), last_rows(vbuf), last_rows(qbuf)
    kv_out[...] = jnp.concatenate(
        [part[:, 1024 * s : 1024 * s + 1024] for s in range(8) for part in (last_k, last_v)], axis=0
    ).astype(BF16)
    q_out[...] = jnp.concatenate([last_q[:, 1024 * s : 1024 * s + 1024] for s in range(8)], axis=0).astype(BF16)
    pl.semaphore_wait(barrier, BLOCKS - 1)
    following = {"ctx": (me + 1) % BLOCKS}
    edge_copies = [
        pltpu.make_async_remote_copy(
            src_ref=src, dst_ref=dst, send_sem=edge_send.at[i], recv_sem=edge_recv.at[i],
            device_id=following, device_id_type=MESH,
        )
        for i, (src, dst) in enumerate([(kv_out, kv_in), (q_out, q_in)])
    ]
    for copy in edge_copies:
        copy.start()
    loads[3].wait()
    inside = jnp.where(me == 0, 0.0, 1.0)
    edge_copies[0].wait_recv()
    arrived = kv_in[...].astype(F32) * inside
    for s in range(8):
        edges[0:4, 1024 * s : 1024 * s + 1024] = arrived[4 * s : 4 * s + 4]

    def tap_rows(which, lanes):
        return [taps[which, i : i + 1, lanes] for i in range(3)]

    def to_channels(h, j):
        to = partner(j)
        return pltpu.make_async_remote_copy(
            src_ref=gated.at[h, to], dst_ref=moved.at[h, me], send_sem=send_one.at[h, to], recv_sem=recv_one.at[h, me],
            device_id={"ctx": to}, device_id_type=MESH,
        )

    for h in range(HALVES):
        def gate(to):
            lanes = pl.ds(pl.multiple_of((HALVES * to + h) * LANES, LANES), LANES)
            fk = featurize(kbuf[:, lanes].astype(F32), tap_rows(1, lanes), edges[0:1, lanes], edges[1:2, lanes])
            fv = featurize(vbuf[:, lanes].astype(F32), tap_rows(2, lanes), edges[2:3, lanes], edges[3:4, lanes])
            return (fk * fv).astype(BF16)

        def gate_and_send(j, carry):
            to = partner(j)
            gated[h, to] = gate(to)
            to_channels(h, j).start()
            return carry

        lax.fori_loop(0, BLOCKS - 1, gate_and_send, 0)
        moved[h, me] = gate(me)

    for i in range(4, 10):
        loads[i].wait()
    for h in range(HALVES):
        lanes = pl.ds(h * LANES, LANES)

        def filter_outer(g):
            rows = pl.ds(pl.multiple_of(16 * g, 16), 16)
            top, low = split(side_by_side(fbuf[:, rows, lanes], BLOCKS))
            turned = dot(t_outer[0], top) + dot(t_outer[1], top) + dot(t_outer[0], low)
            top, low = split(stacked(turned, 2 * BLOCKS))
            spec[:, rows, :] = top
            spec_low[:, rows, :] = low

        loop(8, 2, filter_outer)

        def filter_inner(k):
            slot = pl.ds(pl.multiple_of(2 * k, 2), 2)
            top = spec[slot].reshape(2 * ROWS, LANES)
            low = spec_low[slot].reshape(2 * ROWS, LANES)
            fspec[h, k] = dot(t_inner[0, k], top) + dot(t_inner[1, k], top) + dot(t_inner[0, k], low)

        loop(BLOCKS, 4, filter_inner)

    def to_positions(h, j):
        to = partner(j)
        return pltpu.make_async_remote_copy(
            src_ref=conv.at[h, to], dst_ref=back.at[h, me], send_sem=send_two.at[h, to], recv_sem=recv_two.at[h, me],
            device_id={"ctx": to}, device_id_type=MESH,
        )

    def arrival(src, dst, send, recv, h, origin):
        return pltpu.make_async_remote_copy(
            src_ref=src.at[h, origin], dst_ref=dst.at[h, origin], send_sem=send.at[h, origin],
            recv_sem=recv.at[h, origin], device_id={"ctx": origin}, device_id_type=MESH,
        )

    for h in range(HALVES):
        def await_gated(j, carry):
            arrival(gated, moved, send_one, recv_one, h, (me + j) % BLOCKS).wait_recv()
            return carry

        lax.fori_loop(1, BLOCKS, await_gated, 0)

        def signal_outer(g):
            rows = pl.ds(pl.multiple_of(16 * g, 16), 16)
            pairs = side_by_side(moved[h, :, rows, :].astype(F32), BLOCKS).astype(BF16)
            spec[:, rows, :] = stacked(dot(t_outer[0], pairs), 2 * BLOCKS).astype(BF16)

        loop(8, 2, signal_outer)

        def signal_inner(k):
            slot = pl.ds(pl.multiple_of(2 * k, 2), 2)
            signal = dot(t_inner[0, k], spec[slot].reshape(2 * ROWS, LANES))
            real, imag = signal[:ROWS], signal[ROWS:]
            f_real, f_imag = fspec[h, k, :ROWS], fspec[h, k, ROWS:]
            lone = (lax.broadcasted_iota(jnp.int32, (ROWS, LANES), 0) == 0) & (k == 0)
            f_last = jnp.where(lone, f_imag, f_real)
            f_imag = jnp.where(lone, 0.0, f_imag)
            product = jnp.concatenate([real * f_real - imag * f_imag, real * f_imag + imag * f_last], axis=0)
            mid[slot] = dot(t_inner_back[k], product.astype(BF16)).astype(BF16).reshape(2, ROWS, LANES)

        loop(BLOCKS, 8, signal_inner)
        gain = sbuf[:, h * LANES : (h + 1) * LANES]

        def signal_back(g):
            rows = pl.ds(pl.multiple_of(16 * g, 16), 16)
            pairs = side_by_side(mid[:, rows, :].astype(F32), 2 * BLOCKS).astype(BF16)
            restored = stacked(dot(t_outer_back[...], pairs), BLOCKS)
            conv[h, :, rows, :] = (restored + gain * moved[h, :, rows, :].astype(F32)).astype(BF16)

        loop(8, 2, signal_back)

        def send_back(j, carry):
            to_positions(h, j).start()
            return carry

        lax.fori_loop(0, BLOCKS - 1, send_back, 0)
        back[h, me] = conv[h, me]

    edge_copies[1].wait_recv()
    arrived_q = q_in[...].astype(F32) * inside
    for s in range(8):
        edges[4:6, 1024 * s : 1024 * s + 1024] = arrived_q[2 * s : 2 * s + 2]

    def feature_q(b, carry):
        lanes = pl.ds(pl.multiple_of(b * LANES, LANES), LANES)
        featured[:, lanes] = featurize(
            qbuf[:, lanes].astype(F32), tap_rows(0, lanes), edges[4:5, lanes], edges[5:6, lanes]
        )
        return carry

    lax.fori_loop(0, HALVES * BLOCKS, feature_q, 0)
    for h in range(HALVES):
        def store(origin):
            lanes = pl.ds(pl.multiple_of((HALVES * origin + h) * LANES, LANES), LANES)
            return pltpu.make_async_copy(result.at[:, lanes], out.at[:, lanes], store_sem.at[h, origin])

        def mix(origin):
            lanes = pl.ds(pl.multiple_of((HALVES * origin + h) * LANES, LANES), LANES)
            result[:, lanes] = (featured[:, lanes] * back[h, origin].astype(F32)).astype(BF16)
            store(origin).start()

        mix(me)

        def await_and_mix(j, carry):
            j = 31 - j
            dx, dz, dy = (j % 4), (j // 4) % 2, j // 8
            origin = (((y + 4 - dy) % 4) * 2 + (z + dz) % 2) * 4 + (x + 4 - dx) % 4
            arrival(conv, back, send_two, recv_two, h, origin).wait_recv()
            mix(origin)
            return carry

        lax.fori_loop(0, BLOCKS - 1, await_and_mix, 0)

    for copy in edge_copies:
        copy.wait_send()
    for h in range(HALVES):
        def finish(j, carry):
            to_channels(h, j).wait_send()
            to_positions(h, j).wait_send()
            return carry

        lax.fori_loop(0, BLOCKS - 1, finish, 0)

        def stored(origin, carry):
            lanes = pl.ds(pl.multiple_of((HALVES * origin + h) * LANES, LANES), LANES)
            pltpu.make_async_copy(result.at[:, lanes], out.at[:, lanes], store_sem.at[h, origin]).wait()
            return carry

        lax.fori_loop(0, BLOCKS, stored, 0)


def on_device(query_rows, key_rows, value_rows, short_taps, long_filter, skip_gain):
    rows, width = query_rows.shape
    outer, inner, inner_back, outer_back = transform_tables()
    tables = [high_low(outer), high_low(inner), high(inner_back), high(outer_back)]
    any_spec = pl.BlockSpec(memory_space=pl.ANY)
    dma = pltpu.SemaphoreType.DMA
    blocks = (HALVES, BLOCKS, ROWS, LANES)
    return pl.pallas_call(
        kernel,
        out_shape=jax.ShapeDtypeStruct((rows, width), BF16),
        in_specs=[any_spec] * 10,
        out_specs=any_spec,
        scratch_shapes=[
            pltpu.VMEM((rows, width), BF16), pltpu.VMEM((rows, width), BF16), pltpu.VMEM((rows, width), BF16),
            pltpu.VMEM((3, 3, width), F32), pltpu.VMEM((BLOCKS, ROWS, HALVES * LANES), F32), pltpu.VMEM((1, HALVES * LANES), F32),
            *[pltpu.VMEM(t.shape, BF16) for t in tables],
            pltpu.VMEM((32, 1024), BF16), pltpu.VMEM((32, 1024), BF16), pltpu.VMEM((16, 1024), BF16), pltpu.VMEM((16, 1024), BF16),
            pltpu.VMEM((8, width), F32),
            *[pltpu.VMEM(blocks, BF16)] * 4,
            pltpu.VMEM((2 * BLOCKS, ROWS, LANES), BF16), pltpu.VMEM((2 * BLOCKS, ROWS, LANES), BF16),
            pltpu.VMEM((HALVES, BLOCKS, 2 * ROWS, LANES), F32), pltpu.VMEM((2 * BLOCKS, ROWS, LANES), BF16),
            pltpu.VMEM((rows, width), F32), pltpu.VMEM((rows, width), BF16),
            dma((10,)), dma((2,)), dma((2,)), *[dma((HALVES, BLOCKS))] * 5,
        ],
        compiler_params=pltpu.CompilerParams(collective_id=0, has_side_effects=True, vmem_limit_bytes=62 << 20),
        name="mixer",
    )(
        query_rows, key_rows, value_rows, short_taps, long_filter.reshape(BLOCKS, ROWS, HALVES * LANES),
        skip_gain.reshape(1, HALVES * LANES), *[jnp.asarray(t) for t in tables],
    )


def solution(mesh):
    in_specs = (P(("dp", "ctx"), None), P(("dp", "ctx"), None), P(("dp", "ctx"), None), P(), P(None, "ctx"), P("ctx"))
    return jax.shard_map(on_device, mesh=mesh, in_specs=in_specs, out_specs=P(("dp", "ctx"), None), check_vma=False)
```

time: 361 us -> 71.4 us (0.20); the launches traced: 355 us -> 70.4 us
  matrix products: 143 us -> 0 us
  other arithmetic: 86.6 us -> 0 us
  Pallas kernels: 0 us -> 67.3 us
  local copies, waits for them, and re-layouts: 63.8 us -> 3.1 us
  waiting for transfers between devices: 33.9 us -> 0 us
  starting transfers between devices: 26.7 us -> 0 us
    dot_general x6 -> x0, matrix products: 143 us -> none  [the longest x2 84.9 us: forward_spectrum(): jnp.einsum('pqln,qknc->pklc', inner_pair, turned, precision=lax.Precision...]
    pallas_call x0 -> x1, Pallas kernels: none -> 67.3 us  [on_device(): pl.pallas_call(kernel, out_shape=jax.ShapeDtypeStruct((rows, width), BF16...]
    all_to_all x3 -> x0, waiting for transfers between devices: 33.9 us -> none  [the longest x1 17.9 us: on_device(): lax.all_to_all(key_rows.reshape(row_count, device_count, chan_count), 'ct...]
    sub x2 -> x0, other arithmetic: 28.2 us -> none  [the longest x1 19.5 us: long_convolve(): signal_spec[0] * kernel_spec[0] - signal_spec[1] * kernel_spec[1]]
    convert_element_type x6 -> x0, other arithmetic: 27.8 us -> none  [the longest x1 12.1 us: on_device(): (featured_q * returned.reshape(row_count, total_width).astype(jnp.float32...]
    all_to_all x3 -> x0, starting transfers between devices: 23.6 us -> none  [the longest x1 9.22 us: on_device(): lax.all_to_all(key_rows.reshape(row_count, device_count, chan_count), 'ct...]
    unnamed x29 -> x1, local copies, waits for them, and re-layouts: 23.1 us -> 3.1 us
    dot_general x1 -> x0, local copies, waits for them, and re-layouts: 17.5 us -> none  [inverse_real(): jnp.einsum('pqnl,qklc->pknc', inner_back, spectrum, precision=lax.Precisi...]
  transfers between devices with their start and end apart: 4 -> 0, of which waited for: 3 -> 0; matrix products, arithmetic and copies ran while one was open for 72% -> 0% of each run, Pallas kernels for 0% -> 0%
where the time goes in v1:
time: 71.4 us; the launch traced here: 70.4 us
  Pallas kernels  67.3 us (94%)
  local copies, waits for them, and re-layouts  3.1 us (4%)
    pallas_call x1, Pallas kernels, on_device(): pl.pallas_call(kernel, out_shape=jax.ShapeDtypeStruct((rows, width), BF16...  67.3 us
    unnamed x1, local copies, waits for them, and re-layouts  3.1 us

profile of v1, /device:TPU:1, one launch (start us, length us, event | category | flops | bytes accessed | tf_op | source)
XLA Modules:
  0.0 70.4 jit_solution(11363088246699995919)
XLA Ops:
  0.0 67.3 %mixer.1 = bf16[128,8192]{1,0:T(8,128)(2,1)} custom-call(bf16[128,8192]{1,0:T(8,128)(2,1)} %query.1, bf16[128,8192]{1,0:T(8,128)(2,1)} %key.1, bf16[128,8192]{1,0:T(8,128)(2,1)} %value.1, f32[3,3,8192]{2,1,0:T(4,128)} %short_taps.1, f32[32,128,256]{2,1,0:T(8,128)} %bitcast.2, f32[1,256]{1,0:T(1,128)} %bitcast.3, bf16[2,512,256]{2,1,0:T(8,128)(2,1)} %constant.8.clone.outer, ...), custom_call_target="tpu_custom_call" | custom-call | tf_op jit(solution)/shard_map/mixer/pallas_call | solution.py:326
  67.3 3.1 %copy.12 = bf16[128,8192]{1,0:T(8,128)(2,1)} copy(bf16[128,8192]{1,0:T(8,128)(2,1)} %mixer.1) | data formatting | bytes 4194304

commit v2 on v1

--- a/solution.py
+++ b/solution.py
@@ -95,20 +95,25 @@
     return taps[0] * block + taps[1] * one + taps[2] * two
 
 
+def offsets():
+    span = [(dx, dy, dz) for dy in range(4) for dz in range(2) for dx in range(4)]
+    return sorted(span, key=lambda o: -(min(o[0], 4 - o[0]) + min(o[1], 4 - o[1]) + o[2]))[:-1]
+
+
 def kernel(
     query, key, value, short_taps, filt, skip, outer, inner, inner_back, outer_back, out,
     qbuf, kbuf, vbuf, taps, fbuf, sbuf, t_outer, t_inner, t_inner_back, t_outer_back,
     kv_out, kv_in, q_out, q_in, edges, gated, moved, conv, back,
-    spec, spec_low, fspec, mid, featured, result,
-    load_sem, edge_send, edge_recv, send_one, recv_one, send_two, recv_two, store_sem,
+    spec, spec_low, fspec, mid, featured,
+    load_sem, edge_send, edge_recv, send_one, recv_one, send_top, recv_top, send_two, recv_two,
 ):
     me = lax.axis_index("ctx")
     x, z, y = me % 4, (me // 4) % 2, me // 8
-
-    def partner(j):
-        j = 31 - j
-        dx, dz, dy = (j % 4), (j // 4) % 2, j // 8
-        return (((y + dy) % 4) * 2 + (z + dz) % 2) * 4 + (x + dx) % 4
+    sign = 1 - 2 * (lax.axis_index("dp") % 2)
+
+    def at(offset, way=1):
+        dx, dy, dz = offset
+        return ((y + 4 + way * sign * dy) % 4 * 2 + (z + dz) % 2) * 4 + (x + 4 + way * sign * dx) % 4
 
     barrier = pltpu.get_barrier_semaphore()
 
@@ -122,25 +127,21 @@
         pltpu.make_async_copy(src, dst, load_sem.at[i])
         for i, (src, dst) in enumerate(
             [
-                (key, kbuf), (value, vbuf), (query, qbuf), (short_taps, taps), (filt, fbuf), (outer, t_outer),
+                (key, kbuf), (value, vbuf), (short_taps, taps), (query, qbuf), (filt, fbuf), (outer, t_outer),
                 (inner, t_inner), (skip, sbuf), (inner_back, t_inner_back), (outer_back, t_outer_back),
             ]
         )
     ]
-    for load in loads:
-        load.start()
+    for i in (0, 1, 2):
+        loads[i].start()
     for i in (0, 1, 2):
         loads[i].wait()
+    for i in range(3, 10):
+        loads[i].start()
 
     def last_rows(buf):
         return buf[ROWS - 16 :, :].astype(F32)[14:16]
 
-    last_k, last_v, last_q = last_rows(kbuf), last_rows(vbuf), last_rows(qbuf)
-    kv_out[...] = jnp.concatenate(
-        [part[:, 1024 * s : 1024 * s + 1024] for s in range(8) for part in (last_k, last_v)], axis=0
-    ).astype(BF16)
-    q_out[...] = jnp.concatenate([last_q[:, 1024 * s : 1024 * s + 1024] for s in range(8)], axis=0).astype(BF16)
-    pl.semaphore_wait(barrier, BLOCKS - 1)
     following = {"ctx": (me + 1) % BLOCKS}
     edge_copies = [
         pltpu.make_async_remote_copy(
@@ -149,44 +150,74 @@
         )
         for i, (src, dst) in enumerate([(kv_out, kv_in), (q_out, q_in)])
     ]
-    for copy in edge_copies:
-        copy.start()
-    loads[3].wait()
     inside = jnp.where(me == 0, 0.0, 1.0)
-    edge_copies[0].wait_recv()
-    arrived = kv_in[...].astype(F32) * inside
-    for s in range(8):
-        edges[0:4, 1024 * s : 1024 * s + 1024] = arrived[4 * s : 4 * s + 4]
+    last_k, last_v = last_rows(kbuf), last_rows(vbuf)
+    kv_out[...] = jnp.concatenate(
+        [part[:, 1024 * s : 1024 * s + 1024] for s in range(8) for part in (last_k, last_v)], axis=0
+    ).astype(BF16)
+
+    def lanes_of(owner, h):
+        return pl.ds(pl.multiple_of((HALVES * owner + h) * LANES, LANES), LANES)
 
     def tap_rows(which, lanes):
         return [taps[which, i : i + 1, lanes] for i in range(3)]
 
-    def to_channels(h, j):
-        to = partner(j)
+    def gate(rows, lanes):
+        none = jnp.zeros((1, LANES), F32)
+        before = [edges[i : i + 1, lanes] for i in range(4)] if rows == 16 else [none] * 4
+        fk = featurize(kbuf[:rows, lanes].astype(F32), tap_rows(1, lanes), before[0], before[1])
+        fv = featurize(vbuf[:rows, lanes].astype(F32), tap_rows(2, lanes), before[2], before[3])
+        return (fk * fv).astype(BF16)
+
+    def copy_to(src, dst, send, recv, to, slots, theirs):
         return pltpu.make_async_remote_copy(
-            src_ref=gated.at[h, to], dst_ref=moved.at[h, me], send_sem=send_one.at[h, to], recv_sem=recv_one.at[h, me],
+            src_ref=src, dst_ref=dst, send_sem=send.at[slots], recv_sem=recv.at[theirs],
             device_id={"ctx": to}, device_id_type=MESH,
         )
 
+    def to_channels(h, to, origin):
+        rows = pl.ds(16, ROWS - 16)
+        return copy_to(gated.at[h, to, rows], moved.at[h, origin, rows], send_one, recv_one, to, (h, to), (h, origin))
+
+    def tops(to, origin):
+        rows = pl.ds(0, 16)
+        return copy_to(gated.at[:, to, rows], moved.at[:, origin, rows], send_top, recv_top, to, to, origin)
+
+    def to_positions(h, to, origin):
+        return copy_to(conv.at[h, to], back.at[h, origin], send_two, recv_two, to, (h, to), (h, origin))
+
     for h in range(HALVES):
-        def gate(to):
-            lanes = pl.ds(pl.multiple_of((HALVES * to + h) * LANES, LANES), LANES)
-            fk = featurize(kbuf[:, lanes].astype(F32), tap_rows(1, lanes), edges[0:1, lanes], edges[1:2, lanes])
-            fv = featurize(vbuf[:, lanes].astype(F32), tap_rows(2, lanes), edges[2:3, lanes], edges[3:4, lanes])
-            return (fk * fv).astype(BF16)
-
-        def gate_and_send(j, carry):
-            to = partner(j)
-            gated[h, to] = gate(to)
-            to_channels(h, j).start()
+        def gate_rest(to, carry):
+            gated[h, to, 16:] = gate(ROWS, lanes_of(to, h))[16:]
             return carry
 
-        lax.fori_loop(0, BLOCKS - 1, gate_and_send, 0)
-        moved[h, me] = gate(me)
+        lax.fori_loop(0, BLOCKS, gate_rest, 0)
+        if h == 0:
+            pl.semaphore_wait(barrier, BLOCKS - 1)
+            edge_copies[0].start()
+        for offset in offsets():
+            to_channels(h, at(offset), me).start()
+        if h == 0:
+            edge_copies[0].wait_recv()
+            arrived = kv_in[...].astype(F32) * inside
+            for s in range(8):
+                edges[0:4, 1024 * s : 1024 * s + 1024] = arrived[4 * s : 4 * s + 4]
+
+            def gate_top(to, carry):
+                for half in range(HALVES):
+                    gated[half, to, 0:16] = gate(16, lanes_of(to, half))
+                return carry
+
+            lax.fori_loop(0, BLOCKS, gate_top, 0)
+            for offset in offsets():
+                tops(at(offset), me).start()
+    for h in range(HALVES):
+        moved[h, me] = gated[h, me]
 
     for i in range(4, 10):
         loads[i].wait()
-    for h in range(HALVES):
+
+    def filter_spectrum(h):
         lanes = pl.ds(h * LANES, LANES)
 
         def filter_outer(g):
@@ -203,30 +234,11 @@
             slot = pl.ds(pl.multiple_of(2 * k, 2), 2)
             top = spec[slot].reshape(2 * ROWS, LANES)
             low = spec_low[slot].reshape(2 * ROWS, LANES)
-            fspec[h, k] = dot(t_inner[0, k], top) + dot(t_inner[1, k], top) + dot(t_inner[0, k], low)
+            fspec[k] = dot(t_inner[0, k], top) + dot(t_inner[1, k], top) + dot(t_inner[0, k], low)
 
         loop(BLOCKS, 4, filter_inner)
 
-    def to_positions(h, j):
-        to = partner(j)
-        return pltpu.make_async_remote_copy(
-            src_ref=conv.at[h, to], dst_ref=back.at[h, me], send_sem=send_two.at[h, to], recv_sem=recv_two.at[h, me],
-            device_id={"ctx": to}, device_id_type=MESH,
-        )
-
-    def arrival(src, dst, send, recv, h, origin):
-        return pltpu.make_async_remote_copy(
-            src_ref=src.at[h, origin], dst_ref=dst.at[h, origin], send_sem=send.at[h, origin],
-            recv_sem=recv.at[h, origin], device_id={"ctx": origin}, device_id_type=MESH,
-        )
-
-    for h in range(HALVES):
-        def await_gated(j, carry):
-            arrival(gated, moved, send_one, recv_one, h, (me + j) % BLOCKS).wait_recv()
-            return carry
-
-        lax.fori_loop(1, BLOCKS, await_gated, 0)
-
+    def convolve(h):
         def signal_outer(g):
             rows = pl.ds(pl.multiple_of(16 * g, 16), 16)
             pairs = side_by_side(moved[h, :, rows, :].astype(F32), BLOCKS).astype(BF16)
@@ -238,7 +250,7 @@
             slot = pl.ds(pl.multiple_of(2 * k, 2), 2)
             signal = dot(t_inner[0, k], spec[slot].reshape(2 * ROWS, LANES))
             real, imag = signal[:ROWS], signal[ROWS:]
-            f_real, f_imag = fspec[h, k, :ROWS], fspec[h, k, ROWS:]
+            f_real, f_imag = fspec[k, :ROWS], fspec[k, ROWS:]
             lone = (lax.broadcasted_iota(jnp.int32, (ROWS, LANES), 0) == 0) & (k == 0)
             f_last = jnp.where(lone, f_imag, f_real)
             f_imag = jnp.where(lone, 0.0, f_imag)
@@ -256,17 +268,27 @@
 
         loop(8, 2, signal_back)
 
-        def send_back(j, carry):
-            to_positions(h, j).start()
+    def await_all(arrival):
+        def one(j, carry):
+            arrival((me + j) % BLOCKS).wait_recv()
             return carry
 
-        lax.fori_loop(0, BLOCKS - 1, send_back, 0)
+        lax.fori_loop(1, BLOCKS, one, 0)
+
+    for h in range(HALVES):
+        filter_spectrum(h)
+        if h == 0:
+            await_all(lambda origin: tops(origin, origin))
+        await_all(lambda origin: to_channels(h, origin, origin))
+        convolve(h)
+        for offset in offsets():
+            to_positions(h, at(offset), me).start()
         back[h, me] = conv[h, me]
 
-    edge_copies[1].wait_recv()
-    arrived_q = q_in[...].astype(F32) * inside
-    for s in range(8):
-        edges[4:6, 1024 * s : 1024 * s + 1024] = arrived_q[2 * s : 2 * s + 2]
+    loads[3].wait()
+    last_q = last_rows(qbuf)
+    q_out[...] = jnp.concatenate([last_q[:, 1024 * s : 1024 * s + 1024] for s in range(8)], axis=0).astype(BF16)
+    edge_copies[1].start()
 
     def feature_q(b, carry):
         lanes = pl.ds(pl.multiple_of(b * LANES, LANES), LANES)
@@ -275,45 +297,35 @@
         )
         return carry
 
+    edge_copies[1].wait_recv()
+    arrived_q = q_in[...].astype(F32) * inside
+    for s in range(8):
+        edges[4:6, 1024 * s : 1024 * s + 1024] = arrived_q[2 * s : 2 * s + 2]
     lax.fori_loop(0, HALVES * BLOCKS, feature_q, 0)
+
+    def mix(h, origin):
+        lanes = lanes_of(origin, h)
+        out[:, lanes] = (featured[:, lanes] * back[h, origin].astype(F32)).astype(BF16)
+
     for h in range(HALVES):
-        def store(origin):
-            lanes = pl.ds(pl.multiple_of((HALVES * origin + h) * LANES, LANES), LANES)
-            return pltpu.make_async_copy(result.at[:, lanes], out.at[:, lanes], store_sem.at[h, origin])
-
-        def mix(origin):
-            lanes = pl.ds(pl.multiple_of((HALVES * origin + h) * LANES, LANES), LANES)
-            result[:, lanes] = (featured[:, lanes] * back[h, origin].astype(F32)).astype(BF16)
-            store(origin).start()
-
-        mix(me)
-
-        def await_and_mix(j, carry):
-            j = 31 - j
-            dx, dz, dy = (j % 4), (j // 4) % 2, j // 8
-            origin = (((y + 4 - dy) % 4) * 2 + (z + dz) % 2) * 4 + (x + 4 - dx) % 4
-            arrival(conv, back, send_two, recv_two, h, origin).wait_recv()
-            mix(origin)
-            return carry
-
-        lax.fori_loop(0, BLOCKS - 1, await_and_mix, 0)
+        mix(h, me)
+        for offset in offsets():
+            origin = at(offset, -1)
+            to_positions(h, origin, origin).wait_recv()
+            mix(h, origin)
 
     for copy in edge_copies:
         copy.wait_send()
-    for h in range(HALVES):
-        def finish(j, carry):
-            to_channels(h, j).wait_send()
-            to_positions(h, j).wait_send()
-            return carry
-
-        lax.fori_loop(0, BLOCKS - 1, finish, 0)
-
-        def stored(origin, carry):
-            lanes = pl.ds(pl.multiple_of((HALVES * origin + h) * LANES, LANES), LANES)
-            pltpu.make_async_copy(result.at[:, lanes], out.at[:, lanes], store_sem.at[h, origin]).wait()
-            return carry
-
-        lax.fori_loop(0, BLOCKS, stored, 0)
+
+    def finish(j, carry):
+        to = (me + j) % BLOCKS
+        tops(to, me).wait_send()
+        for h in range(HALVES):
+            to_channels(h, to, me).wait_send()
+            to_positions(h, to, me).wait_send()
+        return carry
+
+    lax.fori_loop(1, BLOCKS, finish, 0)
 
 
 def on_device(query_rows, key_rows, value_rows, short_taps, long_filter, skip_gain):
@@ -325,9 +337,9 @@
     blocks = (HALVES, BLOCKS, ROWS, LANES)
     return pl.pallas_call(
         kernel,
-        out_shape=jax.ShapeDtypeStruct((rows, width), BF16),
+        out_shape=pltpu.VMEM((rows, width), BF16),
         in_specs=[any_spec] * 10,
-        out_specs=any_spec,
+        out_specs=pl.BlockSpec(memory_space=pltpu.VMEM),
         scratch_shapes=[
             pltpu.VMEM((rows, width), BF16), pltpu.VMEM((rows, width), BF16), pltpu.VMEM((rows, width), BF16),
             pltpu.VMEM((3, 3, width), F32), pltpu.VMEM((BLOCKS, ROWS, HALVES * LANES), F32), pltpu.VMEM((1, HALVES * LANES), F32),
@@ -336,11 +348,11 @@
             pltpu.VMEM((8, width), F32),
             *[pltpu.VMEM(blocks, BF16)] * 4,
             pltpu.VMEM((2 * BLOCKS, ROWS, LANES), BF16), pltpu.VMEM((2 * BLOCKS, ROWS, LANES), BF16),
-            pltpu.VMEM((HALVES, BLOCKS, 2 * ROWS, LANES), F32), pltpu.VMEM((2 * BLOCKS, ROWS, LANES), BF16),
-            pltpu.VMEM((rows, width), F32), pltpu.VMEM((rows, width), BF16),
-            dma((10,)), dma((2,)), dma((2,)), *[dma((HALVES, BLOCKS))] * 5,
+            pltpu.VMEM((BLOCKS, 2 * ROWS, LANES), F32), pltpu.VMEM((2 * BLOCKS, ROWS, LANES), BF16),
+            pltpu.VMEM((rows, width), F32),
+            dma((10,)), dma((2,)), dma((2,)), *[dma((HALVES, BLOCKS))] * 2, *[dma((BLOCKS,))] * 2, *[dma((HALVES, BLOCKS))] * 2,
         ],
-        compiler_params=pltpu.CompilerParams(collective_id=0, has_side_effects=True, vmem_limit_bytes=62 << 20),
+        compiler_params=pltpu.CompilerParams(collective_id=0, has_side_effects=True, vmem_limit_bytes=56 << 20),
         name="mixer",
     )(
         query_rows, key_rows, value_rows, short_taps, long_filter.reshape(BLOCKS, ROWS, HALVES * LANES),

time: 71.4 us -> 72 us (level)
  the two profiles are of different devices: /device:TPU:1 before, /device:TPU:34 now
where the time goes in v2:
time: 72 us; the launch traced here: 71.9 us
  Pallas kernels  70.6 us (98%)
  local copies, waits for them, and re-layouts  1.32 us (2%)
    pallas_call x1, Pallas kernels, on_device(): pl.pallas_call(kernel, out_shape=pltpu.VMEM((rows, width), BF16), in_spec...  70.6 us

profile of v2, /device:TPU:34, one launch (start us, length us, event | category | flops | bytes accessed | tf_op | source)
XLA Modules:
  0.0 71.9 jit_solution(4504361214306135719)
XLA Ops:
  0.0 70.6 %mixer.1 = bf16[128,8192]{1,0:T(8,128)(2,1)S(1)} custom-call(bf16[128,8192]{1,0:T(8,128)(2,1)} %query.1, bf16[128,8192]{1,0:T(8,128)(2,1)} %key.1, bf16[128,8192]{1,0:T(8,128)(2,1)} %value.1, f32[3,3,8192]{2,1,0:T(4,128)} %short_taps.1, f32[32,128,256]{2,1,0:T(8,128)} %bitcast.2, f32[1,256]{1,0:T(1,128)} %bitcast.3, ...), custom_call_target="tpu_custom_call" | custom-call | tf_op jit(solution)/shard_map/mixer/pallas_call | solution.py:338
  70.6 1.3 %copy.12 = bf16[128,8192]{1,0:T(8,128)(2,1)} copy(bf16[128,8192]{1,0:T(8,128)(2,1)S(1)} %mixer.1) | data formatting | bytes 4194304

commit v3 on v2

v3 whole, which is shorter than its diff:
```python
import functools

import jax
import jax.numpy as jnp
import ml_dtypes
import numpy as np
from jax import lax
from jax.experimental import pallas as pl
from jax.experimental.pallas import tpu as pltpu
from jax.sharding import PartitionSpec as P

F32, BF16 = jnp.float32, jnp.bfloat16
MESH = pl.DeviceIdType.MESH

BLOCKS, ROWS, LANES = 32, 128, 128
FULL = 2 * BLOCKS * ROWS
HALVES = 2


def transform_tables():
    p, k1 = np.arange(BLOCKS), np.arange(BLOCKS)
    angle = 2 * np.pi * (k1[:, None] * p % 64) / 64
    outer = np.zeros((BLOCKS, 2, BLOCKS))
    outer[:, 0], outer[:, 1] = np.cos(angle), -np.sin(angle)
    outer[0, 1] = np.cos(np.pi * p)
    outer_back = np.zeros((BLOCKS, BLOCKS, 2))
    outer_back[:, :, 0], outer_back[:, :, 1] = 2 * np.cos(angle.T), -2 * np.sin(angle.T)
    outer_back[:, 0, 0], outer_back[:, 0, 1] = 1, np.cos(np.pi * p)
    outer_back /= FULL
    r, k2 = np.arange(ROWS), np.arange(ROWS)
    inner = np.zeros((BLOCKS, 2 * ROWS, 2 * ROWS))
    for k in range(1, BLOCKS):
        turn = 2 * np.pi * ((k + 64 * k2)[:, None] * r % FULL) / FULL
        cos, sin = np.cos(turn), np.sin(turn)
        inner[k] = np.block([[cos, sin], [-sin, cos]])
    half = np.arange(64)[:, None]
    even = 2 * np.pi * (64 * half * r % FULL) / FULL
    odd = 2 * np.pi * ((32 + 64 * half) * r % FULL) / FULL
    inner[0, 0:64, :ROWS], inner[0, 64:128, ROWS:] = np.cos(even), np.cos(odd)
    inner[0, 128:192, :ROWS], inner[0, 192:256, ROWS:] = -np.sin(even), -np.sin(odd)
    inner[0, 128, :ROWS] = np.cos(np.pi * r)
    inner_back = inner.transpose(0, 2, 1).copy()
    weight = np.full(2 * ROWS, 2.0)
    weight[0] = weight[128] = 1
    inner_back[0] *= weight
    eye = np.eye(8)
    outer = np.kron(outer.reshape(2 * BLOCKS, BLOCKS), eye)
    outer_back = np.kron(outer_back.reshape(BLOCKS, 2 * BLOCKS), eye)
    return outer, inner, inner_back, outer_back


def high_low(table):
    table = table.astype(np.float32)
    high = table.astype(ml_dtypes.bfloat16)
    return np.stack([high, (table - high.astype(np.float32)).astype(ml_dtypes.bfloat16)])


def high(table):
    return table.astype(np.float32).astype(ml_dtypes.bfloat16)


def dot(a, b):
    return jnp.dot(a, b, preferred_element_type=F32)


def split(a):
    top = a.astype(BF16)
    return top, (a - top.astype(F32)).astype(BF16)


def side_by_side(x, n):
    return jnp.concatenate([x[:, :8].reshape(8 * n, LANES), x[:, 8:].reshape(8 * n, LANES)], axis=1)


def stacked(z, n):
    return jnp.concatenate([z[:, :LANES].reshape(n, 8, LANES), z[:, LANES:].reshape(n, 8, LANES)], axis=1)


def loop(count, step, body):
    def several(j, carry):
        for i in range(step):
            body(j * step + i)
        return carry

    lax.fori_loop(0, count // step, several, 0)


def featurize(block, taps, edge_two, edge_one):
    row = lax.broadcasted_iota(jnp.int32, (8, LANES), 0)
    one, two = pltpu.roll(block, 1, 0), pltpu.roll(block, 2, 0)
    top_one = jnp.where(row == 0, edge_one, one[:8])
    top_two = jnp.where(row == 0, edge_two, jnp.where(row == 1, edge_one, two[:8]))
    one = jnp.concatenate([top_one, one[8:]], axis=0)
    two = jnp.concatenate([top_two, two[8:]], axis=0)
    return taps[0] * block + taps[1] * one + taps[2] * two


def offsets():
    span = [(dx, dy, dz) for dy in range(4) for dz in range(2) for dx in range(4)]
    return sorted(span, key=lambda o: -(min(o[0], 4 - o[0]) + min(o[1], 4 - o[1]) + o[2]))[:-1]


def kernel(
    query, key, value, short_taps, filt, skip, outer, inner, inner_back, outer_back, out,
    qbuf, kbuf, vbuf, taps, fbuf, sbuf, t_outer, t_inner, t_inner_back, t_outer_back,
    edge_out, edge_in, edges, gated, moved, conv, back, spec, spec_low, fspec,
    load_sem, edge_send, edge_recv, send_one, recv_one, send_two, recv_two,
):
    me = lax.axis_index("ctx")
    x, z, y = me % 4, (me // 4) % 2, me // 8
    sign = 1 - 2 * (lax.axis_index("dp") % 2)

    def at(offset, way=1):
        dx, dy, dz = offset
        return ((y + 4 + way * sign * dy) % 4 * 2 + (z + dz) % 2) * 4 + (x + 4 + way * sign * dx) % 4

    barrier = pltpu.get_barrier_semaphore()

    def greet(j, carry):
        pl.semaphore_signal(barrier, inc=1, device_id={"ctx": (me + j) % BLOCKS}, device_id_type=MESH)
        return carry

    lax.fori_loop(1, BLOCKS, greet, 0)

    loads = [
        pltpu.make_async_copy(src, dst, load_sem.at[i])
        for i, (src, dst) in enumerate(
            [
                (key, kbuf), (value, vbuf), (short_taps, taps), (query, qbuf), (filt, fbuf), (outer, t_outer),
                (inner, t_inner), (skip, sbuf), (inner_back, t_inner_back), (outer_back, t_outer_back),
            ]
        )
    ]
    for i in (0, 1, 2):
        loads[i].start()
    for i in (0, 1, 2):
        loads[i].wait()
    for i in range(3, 10):
        loads[i].start()

    def last_rows(buf, h):
        rows = buf[ROWS - 16 :, :].astype(F32)[14:16]
        picked = [rows[:, (HALVES * b + h) * LANES : (HALVES * b + h + 1) * LANES] for b in range(BLOCKS)]
        return [jnp.concatenate(picked[8 * s : 8 * s + 8], axis=1) for s in range(4)]

    following = {"ctx": (me + 1) % BLOCKS}
    edge_copies = [
        pltpu.make_async_remote_copy(
            src_ref=edge_out.at[i], dst_ref=edge_in.at[i], send_sem=edge_send.at[i], recv_sem=edge_recv.at[i],
            device_id=following, device_id_type=MESH,
        )
        for i in range(3)
    ]
    inside = jnp.where(me == 0, 0.0, 1.0)
    for h in range(HALVES):
        parts = [part for both in zip(last_rows(kbuf, h), last_rows(vbuf, h)) for part in both]
        edge_out[h] = jnp.concatenate(parts, axis=0).astype(BF16)

    def lanes_of(owner, h):
        return pl.ds(pl.multiple_of((HALVES * owner + h) * LANES, LANES), LANES)

    def block_lanes(owner):
        return pl.ds(pl.multiple_of(owner * LANES, LANES), LANES)

    def tap_rows(which, lanes):
        return [taps[which, i : i + 1, lanes] for i in range(3)]

    def gate(rows, owner, h):
        lanes = lanes_of(owner, h)
        if rows == 16:
            before = [edges[h, i : i + 1, block_lanes(owner)] for i in range(4)]
        else:
            before = [jnp.zeros((1, LANES), F32)] * 4
        fk = featurize(kbuf[:rows, lanes].astype(F32), tap_rows(1, lanes), before[0], before[1])
        fv = featurize(vbuf[:rows, lanes].astype(F32), tap_rows(2, lanes), before[2], before[3])
        return (fk * fv).astype(BF16)

    def copy_to(src, dst, send, recv, to, h, origin):
        return pltpu.make_async_remote_copy(
            src_ref=src.at[h, to], dst_ref=dst.at[h, origin], send_sem=send.at[h, to], recv_sem=recv.at[h, origin],
            device_id={"ctx": to}, device_id_type=MESH,
        )

    def to_channels(h, to, origin):
        return copy_to(gated, moved, send_one, recv_one, to, h, origin)

    def to_positions(h, to, origin):
        return copy_to(conv, back, send_two, recv_two, to, h, origin)

    def gate_rest(h):
        def one(owner, carry):
            gated[h, owner, 16:] = gate(ROWS, owner, h)[16:]
            return carry

        lax.fori_loop(0, BLOCKS, one, 0)

    def gate_top(h):
        arrived = edge_in[h].astype(F32) * inside
        for s in range(4):
            edges[h, 0:4, 1024 * s : 1024 * s + 1024] = arrived[4 * s : 4 * s + 4]

        def one(owner, carry):
            gated[h, owner, :16] = gate(16, owner, h)
            return carry

        lax.fori_loop(0, BLOCKS, one, 0)

    gate_rest(0)
    pl.semaphore_wait(barrier, BLOCKS - 1)
    for h in range(HALVES):
        edge_copies[h].start()
    gate_rest(1)
    for h in range(HALVES):
        edge_copies[h].wait_recv()
        gate_top(h)
        for offset in offsets():
            to_channels(h, at(offset), me).start()
    for h in range(HALVES):
        moved[h, me] = gated[h, me]
    loads[3].wait()
    edge_out[2] = jnp.concatenate([part for h in range(HALVES) for part in last_rows(qbuf, h)], axis=0).astype(BF16)
    edge_copies[2].start()

    for i in range(4, 10):
        loads[i].wait()

    def filter_outer(g):
        turned = []
        for i in range(2):
            rows = pl.ds(pl.multiple_of(16 * g + 8 * i, 8), 8)
            top, low = split(fbuf[:, rows, :].reshape(8 * BLOCKS, HALVES * LANES))
            part = dot(t_outer[0], top) + dot(t_outer[1], top) + dot(t_outer[0], low)
            turned.append(part.reshape(2 * BLOCKS, 8, HALVES * LANES))
        top, low = split(jnp.concatenate(turned, axis=1))
        rows = pl.ds(pl.multiple_of(16 * g, 16), 16)
        spec[:, rows, :] = top
        spec_low[:, rows, :] = low

    loop(8, 2, filter_outer)

    def filter_inner(k):
        slot = pl.ds(pl.multiple_of(2 * k, 2), 2)
        top = spec[slot].reshape(2 * ROWS, HALVES * LANES)
        low = spec_low[slot].reshape(2 * ROWS, HALVES * LANES)
        fspec[k] = dot(t_inner[0, k], top) + dot(t_inner[1, k], top) + dot(t_inner[0, k], low)

    loop(BLOCKS, 8, filter_inner)

    edge_copies[2].wait_recv()
    arrived_q = edge_in[2].astype(F32) * inside
    for h in range(HALVES):
        for s in range(4):
            row = 8 * h + 2 * s
            edges[h, 4:6, 1024 * s : 1024 * s + 1024] = arrived_q[row : row + 2]

    def feature_q(owner, carry):
        for h in range(HALVES):
            lanes = lanes_of(owner, h)
            before = [edges[h, i : i + 1, block_lanes(owner)] for i in (4, 5)]
            fbuf[owner, :, h * LANES : (h + 1) * LANES] = featurize(
                qbuf[:, lanes].astype(F32), tap_rows(0, lanes), before[0], before[1]
            )
        return carry

    def convolve(h):
        half = pl.ds(h * LANES, LANES)
        first = pl.ds(0, LANES)

        def signal_outer(g):
            rows = pl.ds(pl.multiple_of(16 * g, 16), 16)
            pairs = side_by_side(moved[h, :, rows, :].astype(F32), BLOCKS).astype(BF16)
            spec[:, rows, first] = stacked(dot(t_outer[0], pairs), 2 * BLOCKS).astype(BF16)

        loop(8, 4, signal_outer)

        def signal_inner(k):
            slot = pl.ds(pl.multiple_of(2 * k, 2), 2)
            signal = dot(t_inner[0, k], spec[slot, :, first].reshape(2 * ROWS, LANES))
            real, imag = signal[:ROWS], signal[ROWS:]
            f_real, f_imag = fspec[k, :ROWS, half], fspec[k, ROWS:, half]
            lone = (lax.broadcasted_iota(jnp.int32, (ROWS, LANES), 0) == 0) & (k == 0)
            f_last = jnp.where(lone, f_imag, f_real)
            f_imag = jnp.where(lone, 0.0, f_imag)
            product = jnp.concatenate([real * f_real - imag * f_imag, real * f_imag + imag * f_last], axis=0)
            restored = dot(t_inner_back[k], product.astype(BF16)).astype(BF16)
            spec_low[slot, :, first] = restored.reshape(2, ROWS, LANES)

        loop(BLOCKS, 8, signal_inner)
        gain = sbuf[:, h * LANES : (h + 1) * LANES]

        def signal_back(g):
            rows = pl.ds(pl.multiple_of(16 * g, 16), 16)
            pairs = side_by_side(spec_low[:, rows, first].astype(F32), 2 * BLOCKS).astype(BF16)
            restored = stacked(dot(t_outer_back[...], pairs), BLOCKS)
            conv[h, :, rows, :] = (restored + gain * moved[h, :, rows, :].astype(F32)).astype(BF16)

        loop(8, 4, signal_back)

    for h in range(HALVES):
        def await_gated(j, carry):
            origin = (me + j) % BLOCKS
            to_channels(h, origin, origin).wait_recv()
            return carry

        lax.fori_loop(1, BLOCKS, await_gated, 0)
        convolve(h)
        for offset in offsets():
            to_positions(h, at(offset), me).start()
        back[h, me] = conv[h, me]

    lax.fori_loop(0, BLOCKS, feature_q, 0)

    def mix(h, origin):
        features = fbuf[origin, :, h * LANES : (h + 1) * LANES]
        out[:, lanes_of(origin, h)] = (features * back[h, origin].astype(F32)).astype(BF16)

    for h in range(HALVES):
        mix(h, me)
        for offset in offsets():
            origin = at(offset, -1)
            to_positions(h, origin, origin).wait_recv()
            mix(h, origin)

    for copy in edge_copies:
        copy.wait_send()

    def finish(j, carry):
        to = (me + j) % BLOCKS
        for h in range(HALVES):
            to_channels(h, to, me).wait_send()
            to_positions(h, to, me).wait_send()
        return carry

    lax.fori_loop(1, BLOCKS, finish, 0)


def on_device(query_rows, key_rows, value_rows, short_taps, long_filter, skip_gain):
    rows, width = query_rows.shape
    outer, inner, inner_back, outer_back = transform_tables()
    tables = [high_low(outer), high_low(inner), high(inner_back), high(outer_back)]
    any_spec = pl.BlockSpec(memory_space=pl.ANY)
    dma = pltpu.SemaphoreType.DMA
    blocks = (HALVES, BLOCKS, ROWS, LANES)
    return pl.pallas_call(
        kernel,
        out_shape=pltpu.VMEM((rows, width), BF16),
        in_specs=[any_spec] * 10,
        out_specs=pl.BlockSpec(memory_space=pltpu.VMEM),
        scratch_shapes=[
            pltpu.VMEM((rows, width), BF16), pltpu.VMEM((rows, width), BF16), pltpu.VMEM((rows, width), BF16),
            pltpu.VMEM((3, 3, width), F32), pltpu.VMEM((BLOCKS, ROWS, HALVES * LANES), F32), pltpu.VMEM((1, HALVES * LANES), F32),
            *[pltpu.VMEM(t.shape, BF16) for t in tables],
            pltpu.VMEM((3, 16, 1024), BF16), pltpu.VMEM((3, 16, 1024), BF16), pltpu.VMEM((HALVES, 8, width // HALVES), F32),
            *[pltpu.VMEM(blocks, BF16)] * 4,
            *[pltpu.VMEM((2 * BLOCKS, ROWS, HALVES * LANES), BF16)] * 2,
            pltpu.VMEM((BLOCKS, 2 * ROWS, HALVES * LANES), F32),
            dma((10,)), dma((3,)), dma((3,)), *[dma((HALVES, BLOCKS))] * 4,
        ],
        compiler_params=pltpu.CompilerParams(collective_id=0, has_side_effects=True, vmem_limit_bytes=56 << 20),
        name="mixer",
    )(
        query_rows, key_rows, value_rows, short_taps, long_filter.reshape(BLOCKS, ROWS, HALVES * LANES),
        skip_gain.reshape(1, HALVES * LANES), *[jnp.asarray(t) for t in tables],
    )


def solution(mesh):
    in_specs = (P(("dp", "ctx"), None), P(("dp", "ctx"), None), P(("dp", "ctx"), None), P(), P(None, "ctx"), P("ctx"))
    return jax.shard_map(on_device, mesh=mesh, in_specs=in_specs, out_specs=P(("dp", "ctx"), None), check_vma=False)
```

time: 72 us -> 70.9 us (0.985)
  the two profiles are of different devices: /device:TPU:34 before, /device:TPU:1 now
where the time goes in v3:
time: 70.9 us; the launch traced here: 69.7 us
  Pallas kernels  68.3 us (96%)
  local copies, waits for them, and re-layouts  1.32 us (2%)
    pallas_call x1, Pallas kernels, on_device(): pl.pallas_call(kernel, out_shape=pltpu.VMEM((rows, width), BF16), in_spec...  68.3 us

profile of v3, /device:TPU:1, one launch (start us, length us, event | category | flops | bytes accessed | tf_op | source)
XLA Modules:
  0.0 69.7 jit_solution(7019898751224655891)
XLA Ops:
  0.0 68.3 %mixer.1 = bf16[128,8192]{1,0:T(8,128)(2,1)S(1)} custom-call(bf16[128,8192]{1,0:T(8,128)(2,1)} %query.1, bf16[128,8192]{1,0:T(8,128)(2,1)} %key.1, bf16[128,8192]{1,0:T(8,128)(2,1)} %value.1, f32[3,3,8192]{2,1,0:T(4,128)} %short_taps.1, f32[32,128,256]{2,1,0:T(8,128)} %bitcast.2, f32[1,256]{1,0:T(1,128)} %bitcast.3, ...), custom_call_target="tpu_custom_call" | custom-call | tf_op jit(solution)/shard_map/mixer/pallas_call | solution.py:344
  68.3 1.3 %copy.12 = bf16[128,8192]{1,0:T(8,128)(2,1)} copy(bf16[128,8192]{1,0:T(8,128)(2,1)S(1)} %mixer.1) | data formatting | bytes 4194304

commit v4 on v3

--- a/solution.py
+++ b/solution.py
@@ -97,7 +97,8 @@
 
 def offsets():
     span = [(dx, dy, dz) for dy in range(4) for dz in range(2) for dx in range(4)]
-    return sorted(span, key=lambda o: -(min(o[0], 4 - o[0]) + min(o[1], 4 - o[1]) + o[2]))[:-1]
+    far = sorted(span, key=lambda o: -(min(o[0], 4 - o[0]) + min(o[1], 4 - o[1]) + o[2]))[:-1]
+    return [far[j // 2] if j % 2 == 0 else far[-1 - j // 2] for j in range(31)]
 
 
 def kernel(
@@ -135,8 +136,7 @@
         loads[i].start()
     for i in (0, 1, 2):
         loads[i].wait()
-    for i in range(3, 10):
-        loads[i].start()
+    loads[4].start()
 
     def last_rows(buf, h):
         rows = buf[ROWS - 16 :, :].astype(F32)[14:16]
@@ -209,19 +209,21 @@
     pl.semaphore_wait(barrier, BLOCKS - 1)
     for h in range(HALVES):
         edge_copies[h].start()
-    gate_rest(1)
-    for h in range(HALVES):
-        edge_copies[h].wait_recv()
-        gate_top(h)
+    loads[5].start()
+    loads[6].start()
+    def send_gated(h):
         for offset in offsets():
             to_channels(h, at(offset), me).start()
-    for h in range(HALVES):
         moved[h, me] = gated[h, me]
-    loads[3].wait()
-    edge_out[2] = jnp.concatenate([part for h in range(HALVES) for part in last_rows(qbuf, h)], axis=0).astype(BF16)
-    edge_copies[2].start()
-
-    for i in range(4, 10):
+
+    edge_copies[0].wait_recv()
+    gate_top(0)
+    send_gated(0)
+    gate_rest(1)
+    edge_copies[1].wait_recv()
+    gate_top(1)
+
+    for i in (4, 5, 6):
         loads[i].wait()
 
     def filter_outer(g):
@@ -237,6 +239,9 @@
         spec_low[:, rows, :] = low
 
     loop(8, 2, filter_outer)
+    for i in (7, 8, 9, 3):
+        loads[i].start()
+    send_gated(1)
 
     def filter_inner(k):
         slot = pl.ds(pl.multiple_of(2 * k, 2), 2)
@@ -246,12 +251,11 @@
 
     loop(BLOCKS, 8, filter_inner)
 
-    edge_copies[2].wait_recv()
-    arrived_q = edge_in[2].astype(F32) * inside
-    for h in range(HALVES):
-        for s in range(4):
-            row = 8 * h + 2 * s
-            edges[h, 4:6, 1024 * s : 1024 * s + 1024] = arrived_q[row : row + 2]
+    loads[3].wait()
+    edge_out[2] = jnp.concatenate([part for h in range(HALVES) for part in last_rows(qbuf, h)], axis=0).astype(BF16)
+    edge_copies[2].start()
+    for i in (7, 8, 9):
+        loads[i].wait()
 
     def feature_q(owner, carry):
         for h in range(HALVES):
@@ -308,6 +312,12 @@
             to_positions(h, at(offset), me).start()
         back[h, me] = conv[h, me]
 
+    edge_copies[2].wait_recv()
+    arrived_q = edge_in[2].astype(F32) * inside
+    for h in range(HALVES):
+        for s in range(4):
+            row = 8 * h + 2 * s
+            edges[h, 4:6, 1024 * s : 1024 * s + 1024] = arrived_q[row : row + 2]
     lax.fori_loop(0, BLOCKS, feature_q, 0)
 
     def mix(h, origin):

time: 70.9 us -> 64.3 us (0.907); the launches traced: 69.7 us -> 64.2 us
  Pallas kernels: 68.3 us -> 62.9 us
    pallas_call x1, Pallas kernels: 68.3 us -> 62.9 us  [on_device(): pl.pallas_call(kernel, out_shape=pltpu.VMEM((rows, width), BF16), in_spec...]
where the time goes in v4:
time: 64.3 us; the launch traced here: 64.2 us
  Pallas kernels  62.9 us (98%)
  local copies, waits for them, and re-layouts  1.32 us (2%)
    pallas_call x1, Pallas kernels, on_device(): pl.pallas_call(kernel, out_shape=pltpu.VMEM((rows, width), BF16), in_spec...  62.9 us
    unnamed x1, local copies, waits for them, and re-layouts  1.32 us

profile of v4, /device:TPU:1, one launch (start us, length us, event | category | flops | bytes accessed | tf_op | source)
XLA Modules:
  0.0 64.2 jit_solution(1162103430624026102)
XLA Ops:
  0.0 62.9 %mixer.1 = bf16[128,8192]{1,0:T(8,128)(2,1)S(1)} custom-call(bf16[128,8192]{1,0:T(8,128)(2,1)} %query.1, bf16[128,8192]{1,0:T(8,128)(2,1)} %key.1, bf16[128,8192]{1,0:T(8,128)(2,1)} %value.1, f32[3,3,8192]{2,1,0:T(4,128)} %short_taps.1, f32[32,128,256]{2,1,0:T(8,128)} %bitcast.2, f32[1,256]{1,0:T(1,128)} %bitcast.3, ...), custom_call_target="tpu_custom_call" | custom-call | tf_op jit(solution)/shard_map/mixer/pallas_call | solution.py:354
  62.9 1.3 %copy.12 = bf16[128,8192]{1,0:T(8,128)(2,1)} copy(bf16[128,8192]{1,0:T(8,128)(2,1)S(1)} %mixer.1) | data formatting | bytes 4194304

commit v5 on v4

--- a/solution.py
+++ b/solution.py
@@ -28,21 +28,23 @@
     outer_back[:, 0, 0], outer_back[:, 0, 1] = 1, np.cos(np.pi * p)
     outer_back /= FULL
     r, k2 = np.arange(ROWS), np.arange(ROWS)
-    inner = np.zeros((BLOCKS, 2 * ROWS, 2 * ROWS))
+    inner = np.zeros((BLOCKS + 1, ROWS, 2 * ROWS))
+    inner_back = np.zeros((BLOCKS + 1, ROWS, 2 * ROWS))
     for k in range(1, BLOCKS):
         turn = 2 * np.pi * ((k + 64 * k2)[:, None] * r % FULL) / FULL
-        cos, sin = np.cos(turn), np.sin(turn)
-        inner[k] = np.block([[cos, sin], [-sin, cos]])
+        inner[k] = np.block([np.cos(turn), np.sin(turn)])
+        inner_back[k] = np.block([np.cos(turn.T), np.sin(turn.T)])
     half = np.arange(64)[:, None]
     even = 2 * np.pi * (64 * half * r % FULL) / FULL
     odd = 2 * np.pi * ((32 + 64 * half) * r % FULL) / FULL
-    inner[0, 0:64, :ROWS], inner[0, 64:128, ROWS:] = np.cos(even), np.cos(odd)
-    inner[0, 128:192, :ROWS], inner[0, 192:256, ROWS:] = -np.sin(even), -np.sin(odd)
-    inner[0, 128, :ROWS] = np.cos(np.pi * r)
-    inner_back = inner.transpose(0, 2, 1).copy()
+    lone = np.zeros((2 * ROWS, 2 * ROWS))
+    lone[0:64, :ROWS], lone[64:128, ROWS:] = np.cos(even), np.cos(odd)
+    lone[128:192, :ROWS], lone[192:256, ROWS:] = -np.sin(even), -np.sin(odd)
+    lone[128, :ROWS] = np.cos(np.pi * r)
     weight = np.full(2 * ROWS, 2.0)
     weight[0] = weight[128] = 1
-    inner_back[0] *= weight
+    inner[0], inner[BLOCKS] = lone[:ROWS], lone[ROWS:]
+    inner_back[0], inner_back[BLOCKS] = (lone.T * weight)[:ROWS], (lone.T * weight)[ROWS:]
     eye = np.eye(8)
     outer = np.kron(outer.reshape(2 * BLOCKS, BLOCKS), eye)
     outer_back = np.kron(outer_back.reshape(BLOCKS, 2 * BLOCKS), eye)
@@ -74,6 +76,25 @@
 
 def stacked(z, n):
     return jnp.concatenate([z[:, :LANES].reshape(n, 8, LANES), z[:, LANES:].reshape(n, 8, LANES)], axis=1)
+
+
+def crossed(real, imag):
+    return jnp.concatenate(
+        [jnp.concatenate([real, imag], axis=1), jnp.concatenate([imag, -real], axis=1)], axis=0
+    )
+
+
+def slots(step, lone, body):
+    lone()
+    for k in range(1, step):
+        body(k)
+
+    def several(j, carry):
+        for i in range(step):
+            body(j * step + i)
+        return carry
+
+    lax.fori_loop(1, BLOCKS // step, several, 0)
 
 
 def loop(count, step, body):
@@ -243,13 +264,23 @@
         loads[i].start()
     send_gated(1)
 
+    def filter_dot(k, top, low):
+        return dot(t_inner[0, k], top) + dot(t_inner[1, k], top) + dot(t_inner[0, k], low)
+
+    def filter_lone():
+        top = spec[0:2].reshape(2 * ROWS, HALVES * LANES)
+        low = spec_low[0:2].reshape(2 * ROWS, HALVES * LANES)
+        fspec[0, :ROWS] = filter_dot(0, top, low)
+        fspec[0, ROWS:] = filter_dot(BLOCKS, top, low)
+
     def filter_inner(k):
-        slot = pl.ds(pl.multiple_of(2 * k, 2), 2)
-        top = spec[slot].reshape(2 * ROWS, HALVES * LANES)
-        low = spec_low[slot].reshape(2 * ROWS, HALVES * LANES)
-        fspec[k] = dot(t_inner[0, k], top) + dot(t_inner[1, k], top) + dot(t_inner[0, k], low)
-
-    loop(BLOCKS, 8, filter_inner)
+        both = filter_dot(
+            k, crossed(spec[2 * k], spec[2 * k + 1]), crossed(spec_low[2 * k], spec_low[2 * k + 1])
+        )
+        fspec[k, :ROWS] = both[:, : HALVES * LANES]
+        fspec[k, ROWS:] = both[:, HALVES * LANES :]
+
+    slots(8, filter_lone, filter_inner)
 
     loads[3].wait()
     edge_out[2] = jnp.concatenate([part for h in range(HALVES) for part in last_rows(qbuf, h)], axis=0).astype(BF16)
@@ -275,21 +306,31 @@
             pairs = side_by_side(moved[h, :, rows, :].astype(F32), BLOCKS).astype(BF16)
             spec[:, rows, first] = stacked(dot(t_outer[0], pairs), 2 * BLOCKS).astype(BF16)
 
-        loop(8, 4, signal_outer)
+        loop(8, 8, signal_outer)
+
+        def signal_lone():
+            signal = spec[0:2, :, first].reshape(2 * ROWS, LANES)
+            real, imag = dot(t_inner[0, 0], signal), dot(t_inner[0, BLOCKS], signal)
+            f_real, f_imag = fspec[0, :ROWS, half], fspec[0, ROWS:, half]
+            top = lax.broadcasted_iota(jnp.int32, (ROWS, LANES), 0) == 0
+            f_last = jnp.where(top, f_imag, f_real)
+            f_imag = jnp.where(top, 0.0, f_imag)
+            product = jnp.concatenate([real * f_real - imag * f_imag, real * f_imag + imag * f_last], axis=0)
+            product = product.astype(BF16)
+            spec_low[0, :, first] = dot(t_inner_back[0], product).astype(BF16)
+            spec_low[1, :, first] = dot(t_inner_back[BLOCKS], product).astype(BF16)
 
         def signal_inner(k):
-            slot = pl.ds(pl.multiple_of(2 * k, 2), 2)
-            signal = dot(t_inner[0, k], spec[slot, :, first].reshape(2 * ROWS, LANES))
-            real, imag = signal[:ROWS], signal[ROWS:]
+            signal = dot(t_inner[0, k], crossed(spec[2 * k, :, first], spec[2 * k + 1, :, first]))
+            real, imag = signal[:, :LANES], signal[:, LANES:]
             f_real, f_imag = fspec[k, :ROWS, half], fspec[k, ROWS:, half]
-            lone = (lax.broadcasted_iota(jnp.int32, (ROWS, LANES), 0) == 0) & (k == 0)
-            f_last = jnp.where(lone, f_imag, f_real)
-            f_imag = jnp.where(lone, 0.0, f_imag)
-            product = jnp.concatenate([real * f_real - imag * f_imag, real * f_imag + imag * f_last], axis=0)
-            restored = dot(t_inner_back[k], product.astype(BF16)).astype(BF16)
-            spec_low[slot, :, first] = restored.reshape(2, ROWS, LANES)
-
-        loop(BLOCKS, 8, signal_inner)
+            up = (real * f_real - imag * f_imag).astype(BF16)
+            across = (real * f_imag + imag * f_real).astype(BF16)
+            restored = dot(t_inner_back[k], crossed(across, up)).astype(BF16)
+            spec_low[2 * k, :, first] = restored[:, LANES:]
+            spec_low[2 * k + 1, :, first] = restored[:, :LANES]
+
+        slots(16, signal_lone, signal_inner)
         gain = sbuf[:, h * LANES : (h + 1) * LANES]
 
         def signal_back(g):
@@ -298,7 +339,7 @@
             restored = stacked(dot(t_outer_back[...], pairs), BLOCKS)
             conv[h, :, rows, :] = (restored + gain * moved[h, :, rows, :].astype(F32)).astype(BF16)
 
-        loop(8, 4, signal_back)
+        loop(8, 8, signal_back)
 
     for h in range(HALVES):
         def await_gated(j, carry):

time: 64.3 us -> 64.7 us (level)
  no operation moved by 1% of the time
where the time goes in v5:
time: 64.7 us; the launch traced here: 64.6 us
  Pallas kernels  63.2 us (98%)
  local copies, waits for them, and re-layouts  1.32 us (2%)
    pallas_call x1, Pallas kernels, on_device(): pl.pallas_call(kernel, out_shape=pltpu.VMEM((rows, width), BF16), in_spec...  63.2 us
    unnamed x1, local copies, waits for them, and re-layouts  1.32 us

profile of v5, /device:TPU:1, one launch (start us, length us, event | category | flops | bytes accessed | tf_op | source)
XLA Modules:
  0.0 64.6 jit_solution(6123274360938283754)
XLA Ops:
  0.0 63.2 %mixer.1 = bf16[128,8192]{1,0:T(8,128)(2,1)S(1)} custom-call(bf16[128,8192]{1,0:T(8,128)(2,1)} %query.1, bf16[128,8192]{1,0:T(8,128)(2,1)} %key.1, bf16[128,8192]{1,0:T(8,128)(2,1)} %value.1, f32[3,3,8192]{2,1,0:T(4,128)} %short_taps.1, f32[32,128,256]{2,1,0:T(8,128)} %bitcast.2, f32[1,256]{1,0:T(1,128)} %bitcast.3, ...), custom_call_target="tpu_custom_call" | custom-call | tf_op jit(solution)/shard_map/mixer/pallas_call | solution.py:395
  63.2 1.3 %copy.12 = bf16[128,8192]{1,0:T(8,128)(2,1)} copy(bf16[128,8192]{1,0:T(8,128)(2,1)S(1)} %mixer.1) | data formatting | bytes 4194304

commit v6 on v5

--- a/solution.py
+++ b/solution.py
@@ -117,16 +117,30 @@
 
 
 def offsets():
+    def hops(o):
+        return min(o[0], 4 - o[0]), min(o[1], 4 - o[1]), o[2]
+
     span = [(dx, dy, dz) for dy in range(4) for dz in range(2) for dx in range(4)]
-    far = sorted(span, key=lambda o: -(min(o[0], 4 - o[0]) + min(o[1], 4 - o[1]) + o[2]))[:-1]
-    return [far[j // 2] if j % 2 == 0 else far[-1 - j // 2] for j in range(31)]
+    left = sorted(span, key=lambda o: -sum(hops(o)))[:-1]
+    order = []
+    while left:
+        order.append(left.pop(0))
+        along = hops(order[-1])
+        rest = [o for o in left if hops(o) == (2 - along[0], 2 - along[1], 1 - along[2])]
+        if rest:
+            left.remove(rest[0])
+            order.append(rest[0])
+    return order
+
+
+EARLY = 16
 
 
 def kernel(
     query, key, value, short_taps, filt, skip, outer, inner, inner_back, outer_back, out,
     qbuf, kbuf, vbuf, taps, fbuf, sbuf, t_outer, t_inner, t_inner_back, t_outer_back,
     edge_out, edge_in, edges, gated, moved, conv, back, spec, spec_low, fspec,
-    load_sem, edge_send, edge_recv, send_one, recv_one, send_two, recv_two,
+    load_sem, edge_send, edge_recv, send_one, recv_one, send_top, recv_top, send_two, recv_two,
 ):
     me = lax.axis_index("ctx")
     x, z, y = me % 4, (me // 4) % 2, me // 8
@@ -135,14 +149,6 @@
     def at(offset, way=1):
         dx, dy, dz = offset
         return ((y + 4 + way * sign * dy) % 4 * 2 + (z + dz) % 2) * 4 + (x + 4 + way * sign * dx) % 4
-
-    barrier = pltpu.get_barrier_semaphore()
-
-    def greet(j, carry):
-        pl.semaphore_signal(barrier, inc=1, device_id={"ctx": (me + j) % BLOCKS}, device_id_type=MESH)
-        return carry
-
-    lax.fori_loop(1, BLOCKS, greet, 0)
 
     loads = [
         pltpu.make_async_copy(src, dst, load_sem.at[i])
@@ -155,6 +161,14 @@
     ]
     for i in (0, 1, 2):
         loads[i].start()
+
+    barrier = pltpu.get_barrier_semaphore()
+
+    def greet(j, carry):
+        pl.semaphore_signal(barrier, inc=1, device_id={"ctx": (me + j) % BLOCKS}, device_id_type=MESH)
+        return carry
+
+    lax.fori_loop(1, BLOCKS, greet, 0)
     for i in (0, 1, 2):
         loads[i].wait()
     loads[4].start()
@@ -205,6 +219,23 @@
     def to_channels(h, to, origin):
         return copy_to(gated, moved, send_one, recv_one, to, h, origin)
 
+    def part_to_channels(rows, send, recv, to, origin):
+        return pltpu.make_async_remote_copy(
+            src_ref=gated.at[0, to, rows], dst_ref=moved.at[0, origin, rows], send_sem=send, recv_sem=recv,
+            device_id={"ctx": to}, device_id_type=MESH,
+        )
+
+    def rest_to_channels(to, origin):
+        return part_to_channels(pl.ds(16, ROWS - 16), send_one.at[0, to], recv_one.at[0, origin], to, origin)
+
+    def top_to_channels(to, origin):
+        return part_to_channels(pl.ds(0, 16), send_top.at[to], recv_top.at[origin], to, origin)
+
+    def first_half(j, to, origin):
+        if j < EARLY:
+            return [rest_to_channels(to, origin), top_to_channels(to, origin)]
+        return [to_channels(0, to, origin)]
+
     def to_positions(h, to, origin):
         return copy_to(conv, back, send_two, recv_two, to, h, origin)
 
@@ -232,14 +263,13 @@
         edge_copies[h].start()
     loads[5].start()
     loads[6].start()
-    def send_gated(h):
-        for offset in offsets():
-            to_channels(h, at(offset), me).start()
-        moved[h, me] = gated[h, me]
-
+    for offset in offsets()[:EARLY]:
+        rest_to_channels(at(offset), me).start()
     edge_copies[0].wait_recv()
     gate_top(0)
-    send_gated(0)
+    for j, offset in enumerate(offsets()):
+        first_half(j, at(offset), me)[-1].start()
+    moved[0, me] = gated[0, me]
     gate_rest(1)
     edge_copies[1].wait_recv()
     gate_top(1)
@@ -262,7 +292,9 @@
     loop(8, 2, filter_outer)
     for i in (7, 8, 9, 3):
         loads[i].start()
-    send_gated(1)
+    for offset in offsets():
+        to_channels(1, at(offset), me).start()
+    moved[1, me] = gated[1, me]
 
     def filter_dot(k, top, low):
         return dot(t_inner[0, k], top) + dot(t_inner[1, k], top) + dot(t_inner[0, k], low)
@@ -342,12 +374,10 @@
         loop(8, 8, signal_back)
 
     for h in range(HALVES):
-        def await_gated(j, carry):
-            origin = (me + j) % BLOCKS
-            to_channels(h, origin, origin).wait_recv()
-            return carry
-
-        lax.fori_loop(1, BLOCKS, await_gated, 0)
+        for j, offset in enumerate(offsets()):
+            origin = at(offset, -1)
+            for copy in first_half(j, origin, origin) if h == 0 else [to_channels(1, origin, origin)]:
+                copy.wait_recv()
         convolve(h)
         for offset in offsets():
             to_positions(h, at(offset), me).start()
@@ -361,6 +391,12 @@
             edges[h, 4:6, 1024 * s : 1024 * s + 1024] = arrived_q[row : row + 2]
     lax.fori_loop(0, BLOCKS, feature_q, 0)
 
+    for j, offset in enumerate(offsets()):
+        for copy in first_half(j, at(offset), me) + [to_channels(1, at(offset), me)]:
+            copy.wait_send()
+    for copy in edge_copies:
+        copy.wait_send()
+
     def mix(h, origin):
         features = fbuf[origin, :, h * LANES : (h + 1) * LANES]
         out[:, lanes_of(origin, h)] = (features * back[h, origin].astype(F32)).astype(BF16)
@@ -371,18 +407,8 @@
             origin = at(offset, -1)
             to_positions(h, origin, origin).wait_recv()
             mix(h, origin)
-
-    for copy in edge_copies:
-        copy.wait_send()
-
-    def finish(j, carry):
-        to = (me + j) % BLOCKS
-        for h in range(HALVES):
-            to_channels(h, to, me).wait_send()
-            to_positions(h, to, me).wait_send()
-        return carry
-
-    lax.fori_loop(1, BLOCKS, finish, 0)
+        for offset in offsets():
+            to_positions(h, at(offset), me).wait_send()
 
 
 def on_device(query_rows, key_rows, value_rows, short_taps, long_filter, skip_gain):
@@ -405,7 +431,7 @@
             *[pltpu.VMEM(blocks, BF16)] * 4,
             *[pltpu.VMEM((2 * BLOCKS, ROWS, HALVES * LANES), BF16)] * 2,
             pltpu.VMEM((BLOCKS, 2 * ROWS, HALVES * LANES), F32),
-            dma((10,)), dma((3,)), dma((3,)), *[dma((HALVES, BLOCKS))] * 4,
+            dma((10,)), dma((3,)), dma((3,)), *[dma((HALVES, BLOCKS))] * 2, *[dma((BLOCKS,))] * 2, *[dma((HALVES, BLOCKS))] * 2,
         ],
         compiler_params=pltpu.CompilerParams(collective_id=0, has_side_effects=True, vmem_limit_bytes=56 << 20),
         name="mixer",

time: 64.7 us -> 64.2 us (level)
  the two profiles are of different devices: /device:TPU:1 before, /device:TPU:2 now
where the time goes in v6:
time: 64.2 us; the launch traced here: 64.1 us
  Pallas kernels  62.8 us (98%)
  local copies, waits for them, and re-layouts  1.32 us (2%)
    pallas_call x1, Pallas kernels, on_device(): pl.pallas_call(kernel, out_shape=pltpu.VMEM((rows, width), BF16), in_spec...  62.8 us
    unnamed x1, local copies, waits for them, and re-layouts  1.32 us

profile of v6, /device:TPU:2, one launch (start us, length us, event | category | flops | bytes accessed | tf_op | source)
XLA Modules:
  0.0 64.1 jit_solution(16281341496089242588)
XLA Ops:
  0.0 62.8 %mixer.1 = bf16[128,8192]{1,0:T(8,128)(2,1)S(1)} custom-call(bf16[128,8192]{1,0:T(8,128)(2,1)} %query.1, bf16[128,8192]{1,0:T(8,128)(2,1)} %key.1, bf16[128,8192]{1,0:T(8,128)(2,1)} %value.1, f32[3,3,8192]{2,1,0:T(4,128)} %short_taps.1, f32[32,128,256]{2,1,0:T(8,128)} %bitcast.2, f32[1,256]{1,0:T(1,128)} %bitcast.3, ...), custom_call_target="tpu_custom_call" | custom-call | tf_op jit(solution)/shard_map/mixer/pallas_call | solution.py:421
  62.8 1.3 %copy.12 = bf16[128,8192]{1,0:T(8,128)(2,1)} copy(bf16[128,8192]{1,0:T(8,128)(2,1)S(1)} %mixer.1) | data formatting | bytes 4194304

commit v7 on v6

--- a/solution.py
+++ b/solution.py
@@ -150,15 +150,21 @@
         dx, dy, dz = offset
         return ((y + 4 + way * sign * dy) % 4 * 2 + (z + dz) % 2) * 4 + (x + 4 + way * sign * dx) % 4
 
+    ends = [
+        pltpu.make_async_copy(src.at[pl.ds(ROWS - 16, 16)], dst.at[pl.ds(ROWS - 16, 16)], load_sem.at[10 + i])
+        for i, (src, dst) in enumerate([(key, kbuf), (value, vbuf)])
+    ]
     loads = [
         pltpu.make_async_copy(src, dst, load_sem.at[i])
         for i, (src, dst) in enumerate(
             [
-                (key, kbuf), (value, vbuf), (short_taps, taps), (query, qbuf), (filt, fbuf), (outer, t_outer),
+                (key.at[pl.ds(0, ROWS - 16)], kbuf.at[pl.ds(0, ROWS - 16)]), (value.at[pl.ds(0, ROWS - 16)], vbuf.at[pl.ds(0, ROWS - 16)]), (short_taps, taps), (query, qbuf), (filt, fbuf), (outer, t_outer),
                 (inner, t_inner), (skip, sbuf), (inner_back, t_inner_back), (outer_back, t_outer_back),
             ]
         )
     ]
+    for load in ends:
+        load.start()
     for i in (0, 1, 2):
         loads[i].start()
 
@@ -169,9 +175,8 @@
         return carry
 
     lax.fori_loop(1, BLOCKS, greet, 0)
-    for i in (0, 1, 2):
-        loads[i].wait()
-    loads[4].start()
+    for load in ends:
+        load.wait()
 
     def last_rows(buf, h):
         rows = buf[ROWS - 16 :, :].astype(F32)[14:16]
@@ -239,12 +244,8 @@
     def to_positions(h, to, origin):
         return copy_to(conv, back, send_two, recv_two, to, h, origin)
 
-    def gate_rest(h):
-        def one(owner, carry):
-            gated[h, owner, 16:] = gate(ROWS, owner, h)[16:]
-            return carry
-
-        lax.fori_loop(0, BLOCKS, one, 0)
+    def gate_rest(h, owner):
+        gated[h, owner, 16:] = gate(ROWS, owner, h)[16:]
 
     def gate_top(h):
         arrived = edge_in[h].astype(F32) * inside
@@ -257,20 +258,30 @@
 
         lax.fori_loop(0, BLOCKS, one, 0)
 
-    gate_rest(0)
+    for i in (0, 1, 2):
+        loads[i].wait()
     pl.semaphore_wait(barrier, BLOCKS - 1)
     for h in range(HALVES):
         edge_copies[h].start()
-    loads[5].start()
-    loads[6].start()
     for offset in offsets()[:EARLY]:
+        gate_rest(0, at(offset))
         rest_to_channels(at(offset), me).start()
+    for i in (4, 5, 6):
+        loads[i].start()
+    for offset in offsets()[EARLY:]:
+        gate_rest(0, at(offset))
+    gate_rest(0, me)
     edge_copies[0].wait_recv()
     gate_top(0)
     for j, offset in enumerate(offsets()):
         first_half(j, at(offset), me)[-1].start()
     moved[0, me] = gated[0, me]
-    gate_rest(1)
+
+    def gate_second(owner, carry):
+        gate_rest(1, owner)
+        return carry
+
+    lax.fori_loop(0, BLOCKS, gate_second, 0)
     edge_copies[1].wait_recv()
     gate_top(1)
 
@@ -431,7 +442,7 @@
             *[pltpu.VMEM(blocks, BF16)] * 4,
             *[pltpu.VMEM((2 * BLOCKS, ROWS, HALVES * LANES), BF16)] * 2,
             pltpu.VMEM((BLOCKS, 2 * ROWS, HALVES * LANES), F32),
-            dma((10,)), dma((3,)), dma((3,)), *[dma((HALVES, BLOCKS))] * 2, *[dma((BLOCKS,))] * 2, *[dma((HALVES, BLOCKS))] * 2,
+            dma((12,)), dma((3,)), dma((3,)), *[dma((HALVES, BLOCKS))] * 2, *[dma((BLOCKS,))] * 2, *[dma((HALVES, BLOCKS))] * 2,
         ],
         compiler_params=pltpu.CompilerParams(collective_id=0, has_side_effects=True, vmem_limit_bytes=56 << 20),
         name="mixer",

time: 64.2 us -> 61.4 us (0.956)
  the two profiles are of different devices: /device:TPU:2 before, /device:TPU:1 now
where the time goes in v7:
time: 61.4 us; the launch traced here: 61.3 us
  Pallas kernels  60 us (98%)
  local copies, waits for them, and re-layouts  1.32 us (2%)
    pallas_call x1, Pallas kernels, on_device(): pl.pallas_call(kernel, out_shape=pltpu.VMEM((rows, width), BF16), in_spec...  60 us
    unnamed x1, local copies, waits for them, and re-layouts  1.32 us

profile of v7, /device:TPU:1, one launch (start us, length us, event | category | flops | bytes accessed | tf_op | source)
XLA Modules:
  0.0 61.3 jit_solution(17235735105449367762)
XLA Ops:
  0.0 60.0 %mixer.1 = bf16[128,8192]{1,0:T(8,128)(2,1)S(1)} custom-call(bf16[128,8192]{1,0:T(8,128)(2,1)} %query.1, bf16[128,8192]{1,0:T(8,128)(2,1)} %key.1, bf16[128,8192]{1,0:T(8,128)(2,1)} %value.1, f32[3,3,8192]{2,1,0:T(4,128)} %short_taps.1, f32[32,128,256]{2,1,0:T(8,128)} %bitcast.2, f32[1,256]{1,0:T(1,128)} %bitcast.3, ...), custom_call_target="tpu_custom_call" | custom-call | tf_op jit(solution)/shard_map/mixer/pallas_call | solution.py:432
  60.0 1.3 %copy.12 = bf16[128,8192]{1,0:T(8,128)(2,1)} copy(bf16[128,8192]{1,0:T(8,128)(2,1)S(1)} %mixer.1) | data formatting | bytes 4194304

commit v8 on v7

--- a/solution.py
+++ b/solution.py
@@ -130,10 +130,10 @@
         if rest:
             left.remove(rest[0])
             order.append(rest[0])
-    return order
-
-
-EARLY = 16
+    return sorted(order, key=lambda o: o[1] % 2)
+
+
+EARLY = 15
 
 
 def kernel(
@@ -154,19 +154,29 @@
         pltpu.make_async_copy(src.at[pl.ds(ROWS - 16, 16)], dst.at[pl.ds(ROWS - 16, 16)], load_sem.at[10 + i])
         for i, (src, dst) in enumerate([(key, kbuf), (value, vbuf)])
     ]
+    def quarter(src, dst, dy, slot):
+        width = src.shape[1] // 4
+        part = (pl.ds(0, ROWS - 16), pl.ds(pl.multiple_of((y + dy) % 4 * width, width), width))
+        return pltpu.make_async_copy(src.at[part], dst.at[part], load_sem.at[slot])
+
+    quarters = [
+        quarter(src, dst, dy, 12 + 2 * i + n)
+        for i, dy in enumerate((2, 0, 1, 3))
+        for n, (src, dst) in enumerate([(key, kbuf), (value, vbuf)])
+    ]
     loads = [
-        pltpu.make_async_copy(src, dst, load_sem.at[i])
+        pltpu.make_async_copy(src, dst, load_sem.at[i + 2])
         for i, (src, dst) in enumerate(
             [
-                (key.at[pl.ds(0, ROWS - 16)], kbuf.at[pl.ds(0, ROWS - 16)]), (value.at[pl.ds(0, ROWS - 16)], vbuf.at[pl.ds(0, ROWS - 16)]), (short_taps, taps), (query, qbuf), (filt, fbuf), (outer, t_outer),
+                (short_taps, taps), (query, qbuf), (filt, fbuf), (outer, t_outer),
                 (inner, t_inner), (skip, sbuf), (inner_back, t_inner_back), (outer_back, t_outer_back),
             ]
         )
     ]
     for load in ends:
         load.start()
-    for i in (0, 1, 2):
-        loads[i].start()
+    for load in [loads[0], *quarters]:
+        load.start()
 
     barrier = pltpu.get_barrier_semaphore()
 
@@ -258,16 +268,18 @@
 
         lax.fori_loop(0, BLOCKS, one, 0)
 
-    for i in (0, 1, 2):
-        loads[i].wait()
+    for load in [loads[0], *quarters[:4]]:
+        load.wait()
     pl.semaphore_wait(barrier, BLOCKS - 1)
     for h in range(HALVES):
         edge_copies[h].start()
     for offset in offsets()[:EARLY]:
         gate_rest(0, at(offset))
         rest_to_channels(at(offset), me).start()
-    for i in (4, 5, 6):
+    for i in (2, 3, 4):
         loads[i].start()
+    for load in quarters[4:]:
+        load.wait()
     for offset in offsets()[EARLY:]:
         gate_rest(0, at(offset))
     gate_rest(0, me)
@@ -285,7 +297,7 @@
     edge_copies[1].wait_recv()
     gate_top(1)
 
-    for i in (4, 5, 6):
+    for i in (2, 3, 4):
         loads[i].wait()
 
     def filter_outer(g):
@@ -301,7 +313,7 @@
         spec_low[:, rows, :] = low
 
     loop(8, 2, filter_outer)
-    for i in (7, 8, 9, 3):
+    for i in (5, 6, 7, 1):
         loads[i].start()
     for offset in offsets():
         to_channels(1, at(offset), me).start()
@@ -325,10 +337,10 @@
 
     slots(8, filter_lone, filter_inner)
 
-    loads[3].wait()
+    loads[1].wait()
     edge_out[2] = jnp.concatenate([part for h in range(HALVES) for part in last_rows(qbuf, h)], axis=0).astype(BF16)
     edge_copies[2].start()
-    for i in (7, 8, 9):
+    for i in (5, 6, 7):
         loads[i].wait()
 
     def feature_q(owner, carry):
@@ -442,7 +454,7 @@
             *[pltpu.VMEM(blocks, BF16)] * 4,
             *[pltpu.VMEM((2 * BLOCKS, ROWS, HALVES * LANES), BF16)] * 2,
             pltpu.VMEM((BLOCKS, 2 * ROWS, HALVES * LANES), F32),
-            dma((12,)), dma((3,)), dma((3,)), *[dma((HALVES, BLOCKS))] * 2, *[dma((BLOCKS,))] * 2, *[dma((HALVES, BLOCKS))] * 2,
+            dma((20,)), dma((3,)), dma((3,)), *[dma((HALVES, BLOCKS))] * 2, *[dma((BLOCKS,))] * 2, *[dma((HALVES, BLOCKS))] * 2,
         ],
         compiler_params=pltpu.CompilerParams(collective_id=0, has_side_effects=True, vmem_limit_bytes=56 << 20),
         name="mixer",

time: 61.4 us -> 62.2 us (1.013)
  Pallas kernels: 60 us -> 60.7 us
    pallas_call x1, Pallas kernels: 60 us -> 60.7 us  [on_device(): pl.pallas_call(kernel, out_shape=pltpu.VMEM((rows, width), BF16), in_spec...]
where the time goes in v8:
time: 62.2 us; the launch traced here: 62.1 us
  Pallas kernels  60.7 us (98%)
  local copies, waits for them, and re-layouts  1.32 us (2%)
    pallas_call x1, Pallas kernels, on_device(): pl.pallas_call(kernel, out_shape=pltpu.VMEM((rows, width), BF16), in_spec...  60.7 us
    unnamed x1, local copies, waits for them, and re-layouts  1.32 us

profile of v8, /device:TPU:1, one launch (start us, length us, event | category | flops | bytes accessed | tf_op | source)
XLA Modules:
  0.0 62.1 jit_solution(4151592753305951415)
XLA Ops:
  0.0 60.7 %mixer.1 = bf16[128,8192]{1,0:T(8,128)(2,1)S(1)} custom-call(bf16[128,8192]{1,0:T(8,128)(2,1)} %query.1, bf16[128,8192]{1,0:T(8,128)(2,1)} %key.1, bf16[128,8192]{1,0:T(8,128)(2,1)} %value.1, f32[3,3,8192]{2,1,0:T(4,128)} %short_taps.1, f32[32,128,256]{2,1,0:T(8,128)} %bitcast.2, f32[1,256]{1,0:T(1,128)} %bitcast.3, ...), custom_call_target="tpu_custom_call" | custom-call | tf_op jit(solution)/shard_map/mixer/pallas_call | solution.py:444
  60.7 1.3 %copy.12 = bf16[128,8192]{1,0:T(8,128)(2,1)} copy(bf16[128,8192]{1,0:T(8,128)(2,1)S(1)} %mixer.1) | data formatting | bytes 4194304
